TPU v7x, 32 devices: a whole 2x2x4 slice. The times are simulated.
32 devices in a mesh: lon: 8 (over z, y), lat: 4 (over x, core).
Axes of the slice: x: 2, y: 2, z: 4, core: 2. Of those that a mesh axis runs over, the one named last changes fastest.
Arguments:
- wind_u: float32 [720, 1440, 16], P('lat', 'lon'), may hold values from -6 to 6
- wind_v: float32 [720, 1440, 16], P('lat', 'lon'), may hold values from -6 to 6
- vorticity: float32 [720, 1440, 16], P('lat', 'lon'), may hold values from -6 to 6
- sample_level: int32 [16], replicated, may hold values from 0 to 1, as said below
- slot_wavenumber: int32 [720], P('lon'), may hold values from 0 to 719, as said below
- legendre_p: bfloat16 [720, 518400], P('lat', 'lon'), may hold values from -5 to 5
- legendre_h: bfloat16 [720, 518400], P('lat', 'lon'), may hold values from -5 to 5
Outputs:
- spectra: float32 [2, 518400], P(None, ('lon', 'lat'))
Inputs may be any that keep to these rules, and one draw needn't show every extreme that they name: `sample_level`: each level is named by exactly 8 samples. `slot_wavenumber`: each wavenumber from 0 to 719 stands in exactly one slot; the remaining slots hold -1.
All inputs are finite; a program needn't handle non-finite values.
Results may differ from a plain program's by a relative error of at most 0.0014.
Values sent between devices are 32-bit elements; how exact they have to be, the bound alone decides.
No kernel may reach another device: no remote copies, remote signals or barrier semaphores. Data moves between devices by JAX's collectives and lax.ppermute only.
A program may use at most 192 MiB of HBM per device.

v0:
```python
import math

import jax
import jax.numpy as jnp
from jax import lax
from jax.sharding import PartitionSpec as P

NLON = 1440
NLAT = 720
MAXM = 720
LEV = 2
DAYS = 8
S = 16


def remove_means(field, onehot):
    means = jnp.einsum("jis,sl->jil", field, onehot, precision=lax.Precision.HIGHEST) / DAYS
    return field - jnp.einsum("jil,sl->jis", means, onehot, precision=lax.Precision.HIGHEST)


def fourier_table(waves, count):
    longitude = jnp.arange(count, dtype=jnp.int32)
    present = waves >= 0
    clipped = jnp.maximum(waves, 0)
    residue = longitude[:, None] * clipped[None, :] % NLON
    angle = residue.astype(jnp.float32) * (2.0 * math.pi / NLON)
    weight = present.astype(jnp.float32)[None, :] / NLON
    return jnp.stack([jnp.cos(angle) * weight, jnp.sin(angle) * weight], axis=2)


def body(wind_u, wind_v, vorticity, sample_level, slot_wavenumber, legendre_p, legendre_h):
    band_rows = wind_u.shape[0]
    lat_count = lax.axis_size("lat")
    onehot = (sample_level[:, None] == jnp.arange(LEV, dtype=jnp.int32)[None, :]).astype(
        jnp.float32
    )
    eddy_u = remove_means(wind_u, onehot)
    eddy_v = remove_means(wind_v, onehot)
    eddy_z = remove_means(vorticity, onehot)
    row_index = lax.axis_index("lat") * band_rows + jnp.arange(band_rows, dtype=jnp.int32)
    latitude = (row_index.astype(jnp.float32) + 0.5) * (math.pi / NLAT) - 0.5 * math.pi
    cosine = jnp.cos(latitude)[:, None, None]
    fluxes = jnp.concatenate([eddy_u * eddy_z * cosine, eddy_v * eddy_z * cosine], axis=2)
    owned_count = slot_wavenumber.shape[0]
    every_slot = lax.all_gather(slot_wavenumber, "lon", axis=0, tiled=True)
    circles = lax.all_to_all(fluxes, "lon", split_axis=2, concat_axis=1, tiled=True)
    table = fourier_table(every_slot, circles.shape[1])
    spectral = jnp.einsum("jic,iqt->jqtc", circles, table, precision=lax.Precision.HIGHEST)
    coeffs = lax.all_to_all(spectral, "lon", split_axis=1, concat_axis=3, tiled=True)
    present = slot_wavenumber >= 0
    clipped = jnp.maximum(slot_wavenumber, 0)
    scale = (clipped.astype(jnp.float32) / MAXM)[None, :, None]
    cos_u = coeffs[:, :, 0, :S]
    sin_u = coeffs[:, :, 1, :S]
    cos_v = coeffs[:, :, 0, S:]
    sin_v = coeffs[:, :, 1, S:]
    right_p = jnp.concatenate([scale * sin_u, scale * cos_u], axis=2).astype(jnp.bfloat16)
    right_h = jnp.concatenate([-cos_v, sin_v], axis=2).astype(jnp.bfloat16)
    table_p = legendre_p.reshape(band_rows, owned_count, MAXM)
    table_h = legendre_h.reshape(band_rows, owned_count, MAXM)
    partial_sum = jnp.einsum("jqn,jqc->qnc", table_p, right_p, preferred_element_type=jnp.float32)
    partial_sum = partial_sum + jnp.einsum(
        "jqn,jqc->qnc", table_h, right_h, preferred_element_type=jnp.float32
    )
    degree = jnp.arange(MAXM, dtype=jnp.int32)
    keep = ((degree[None, :] >= clipped[:, None]) & present[:, None]).astype(jnp.float32)
    flat_terms = (partial_sum * keep[:, :, None]).reshape(owned_count * MAXM, 2 * S)
    share = flat_terms.shape[0] // lat_count
    summed = lax.psum(flat_terms, "lat")
    mine = lax.dynamic_slice_in_dim(summed, lax.axis_index("lat") * share, share, 0)
    power = mine[:, :S] ** 2 + mine[:, S:] ** 2
    spectra = jnp.dot(power, onehot, precision=lax.Precision.HIGHEST) / DAYS
    return spectra.T


def solution(mesh):
    placed = (
        P("lat", "lon", None),
        P("lat", "lon", None),
        P("lat", "lon", None),
        P(),
        P("lon"),
        P("lat", "lon"),
        P("lat", "lon"),
    )
    return jax.shard_map(
        body, mesh=mesh, in_specs=placed, out_specs=P(None, ("lon", "lat")), check_vma=False
    )
```

profile of v0, /device:TPU:0, one launch (start us, length us, event | category | flops | bytes accessed | tf_op | source)
XLA Modules:
  0.0 631.0 jit_solution(12965043084813032958)
XLA Ops:
  6.6 3.1 fusion.27
  9.8 2.5 convolution_subtract_fusion
  12.2 1.1 fusion.26
  13.4 1.1 fusion.28
  14.5 1.9 multiply_multiply_fusion
  16.4 1.9 multiply_multiply_fusion.1
  18.3 0.8 pad_maximum_fusion
  19.2 6.2 copy.17
  25.4 7.4 %all-to-all-start = ((f32[180,180,32]{1,0,2:T(8,128)}), f32[180,180,32]{1,0,2:T(8,128)}, u32[]{:S(2)}, u32[]{:S(2)}) async-start(f32[180,180,32]{1,0,2:T(8,128)} %copy.17), calls=%async_computation | async-start | bytes 12058624 | tf_op jit(solution)/shard_map/all_to_all | solution.py:46
  32.8 0.6 dynamic-slice
  34.3 131.2 %all-reduce = s32[720]{0:T(1024)S(1)} all-reduce(s32[720]{0:T(1024)S(1)} %dynamic-update-slice), channel_id=1, replica_groups=mesh['lon'=8,'lat'=4] {'lon'}, use_global_device_ids=true, to_apply=%add | all-reduce | flops 720 | bytes 5760
  165.5 20.2 %cosine_multiply_fusion = (f32[1440,720,1]{1,0,2:T(8,128)}, f32[1440,720,1]{1,0,2:T(8,128)}) fusion(f32[720]{0:T(1024)S(1)} %compare_select_fusion, s32[720]{0:T(1024)S(1)} %broadcast_maximum_fusion), kind=kLoop, calls=%fused_computation.16 | loop fusion | flops 11404800 | bytes 8300160 | tf_op jit(solution)/shard_map/mul | solution.py:28
  185.8 8.7 %copy.34 = f32[180,180,8,4]{1,2,0,3:T(8,128)} copy(f32[180,180,8,4]{1,0,3,2:T(8,128)} %bitcast.7) | data formatting | bytes 8294400 | tf_op jit(solution)/shard_map/all_to_all | solution.py:46
  194.4 6.6 %reshape.189 = f32[180,1440,4,1]{1,0,2,3:T(8,128)} reshape(f32[180,8,180,4]{2,1,0,3:T(8,128)} %bitcast.68) | data formatting | bytes 8294400 | tf_op jit(solution)/shard_map/all_to_all | solution.py:46
  201.0 26.6 %fusion.14 = f32[180,720,2,4]{1,0,3,2:T(8,128)} fusion(f32[180,1440,4,1]{1,0,2,3:T(8,128)} %reshape.189, f32[1440,720,1]{1,0,2:T(8,128)} %get-tuple-element.8, f32[1440,720,1]{1,0,2:T(8,128)} %get-tuple-element.7), kind=kOutput, calls=%fused_computation.23 | convolution fusion | flops 17917976576 | bytes 16588800 | tf_op jit(solution)/shard_map/jic,iqt->jqtc/dot_general | solution.py:48
  227.6 7.0 %copy.19 = f32[180,720,2,4]{0,3,2,1:T(4,128)} copy(f32[180,720,2,4]{1,0,3,2:T(8,128)} %fusion.14) | data formatting | bytes 8294400 | tf_op jit(solution)/shard_map/jic,iqt->jqtc/transpose | solution.py:48
  234.7 4.7 all-to-all-start.1
  239.4 51.6 %reshape.180 = bf16[180,90,720]{2,1,0:T(8,128)(2,1)} reshape(bf16[180,64800]{1,0:T(8,128)(2,1)} %param.13) | data formatting | bytes 46656000 | tf_op jit(solution)/shard_map/reshape | solution.py:60
  291.1 51.2 %reshape.179 = bf16[180,90,720]{2,1,0:T(8,128)(2,1)} reshape(bf16[180,64800]{1,0:T(8,128)(2,1)} %param.12) | data formatting | bytes 46656000 | tf_op jit(solution)/shard_map/reshape | solution.py:59
  342.4 25.9 %all-to-all-done.1 = f32[180,720,2,4]{0,3,2,1:T(4,128)} async-done(((f32[180,720,2,4]{0,3,2,1:T(4,128)}), f32[180,720,2,4]{0,3,2,1:T(4,128)}, u32[]{:S(2)}, u32[]{:S(2)}) %all-to-all-start.1) | async-done | bytes 4147232 | tf_op jit(solution)/shard_map/all_to_all | solution.py:49
  368.3 6.8 %copy.26 = f32[180,8,90,2,4]{2,1,0,4,3:T(8,128)} copy(f32[180,8,90,2,4]{0,4,3,2,1:T(4,128)} %bitcast.10) | data formatting | bytes 8294400 | tf_op jit(solution)/shard_map/all_to_all | solution.py:49
  375.1 8.4 %copy.21 = f32[180,90,2,8,4]{0,4,3,1,2:T(4,128)} copy(f32[180,90,2,8,4]{1,3,0,4,2:T(8,128)} %bitcast.69) | data formatting | bytes 8294400 | tf_op jit(solution)/shard_map/all_to_all | solution.py:49
  383.5 7.5 %all_to_all.33 = f32[180,90,2,32]{0,3,1,2:T(8,128)} reshape(f32[180,90,2,8,4]{0,4,3,1,2:T(4,128)} %copy.21) | data formatting | bytes 8294400 | tf_op jit(solution)/shard_map/all_to_all | solution.py:49
  391.0 1.6 fusion.31
  392.6 1.5 fusion.32
  394.1 2.1 fusion.19
  396.2 29.6 %fusion = f32[90,32,720]{2,1,0:T(8,128)} fusion(bf16[180,90,720]{2,1,0:T(8,128)(2,1)} %reshape.180, bf16[180,90,16]{0,2,1:T(8,128)(2,1)S(1)} %fusion.32, bf16[180,90,16]{0,2,1:T(8,128)(2,1)S(1)} %fusion.31), kind=kOutput, calls=%fused_computation | convolution fusion | flops 748569600 | bytes 32659200 | tf_op jit(solution)/shard_map/jqn,jqc->qnc/dot_general | solution.py:62
  425.8 25.4 %multiply_bitcast_fusion = f32[90,720,32]{1,2,0:T(8,128)S(1)} fusion(f32[90,32,720]{2,1,0:T(8,128)} %fusion, f32[90,720]{1,0:T(8,128)S(1)} %fusion.34, bf16[180,90,720]{2,1,0:T(8,128)(2,1)} %reshape.179, bf16[180,90,16]{0,2,1:T(8,128)(2,1)S(1)} %get-tuple-element.6, bf16[180,90,16]{0,2,1:T(8,128)(2,1)S(1)} %get-tuple-element.5), kind=kOutput, calls=%fused_computation.9 | convolution fusion | flops 752716800 | bytes 41212800 | tf_op jit(solution)/shard_map/jqn,jqc->qnc/dot_general | solution.py:61
  451.2 8.8 %copy.24 = f32[90,720,32]{1,0,2:T(8,128)} copy(f32[90,720,32]{1,2,0:T(8,128)S(1)} %multiply_bitcast_fusion) | data formatting | bytes 16588800 | tf_op jit(solution)/shard_map/mul | solution.py:67
  460.0 9.7 %reshape.181 = f32[64800,32]{0,1:T(8,128)} reshape(f32[90,720,32]{1,0,2:T(8,128)} %copy.24) | data formatting | bytes 16588800 | tf_op jit(solution)/shard_map/reshape | solution.py:67
  469.7 150.9 %all-reduce.3.cloned.1.call-done = f32[64800,32]{0,1:T(8,128)} async-done(((f32[64800,32]{0,1:T(8,128)}), f32[64800,32]{0,1:T(8,128)}) %all-reduce.3.cloned.1.call-update) | async-done | bytes 8294416 | tf_op jit(solution)/shard_map/psum | solution.py:69
  620.6 3.1 convolution_multiply_fusion
  (24 shorter events, 0.5 us)
Async XLA Ops:
  6.5 3.2 copy-start
  6.6 5.6 copy-start.1
  6.6 5.6 copy-start.3
  9.8 3.6 copy-start.2
  25.4 7.4 %copy-start.5 = (u32[32]{0:T(128)S(1)}, u32[32]{0:T(128)}, u32[]{:S(2)}) copy-start(u32[32]{0:T(128)} %constant.54) | copy-start | bytes 388
  25.4 8.7 %copy-start.4 = (s32[90]{0:T(128)S(1)}, s32[90]{0:T(128)}, u32[]{:S(2)}) copy-start(s32[90]{0:T(128)} %param.11) | copy-start | bytes 1084
  25.4 160.4 %all-to-all-start = ((f32[180,180,32]{1,0,2:T(8,128)}), f32[180,180,32]{1,0,2:T(8,128)}, u32[]{:S(2)}, u32[]{:S(2)}) async-start(f32[180,180,32]{1,0,2:T(8,128)} %copy.17), calls=%async_computation | async-start | bytes 12058624 | tf_op jit(solution)/shard_map/all_to_all | solution.py:46
  234.7 133.7 %all-to-all-start.1 = ((f32[180,720,2,4]{0,3,2,1:T(4,128)}), f32[180,720,2,4]{0,3,2,1:T(4,128)}, u32[]{:S(2)}, u32[]{:S(2)}) async-start(f32[180,720,2,4]{0,3,2,1:T(4,128)} %copy.19), calls=%async_computation.1 | async-start | bytes 11796480 | tf_op jit(solution)/shard_map/all_to_all | solution.py:49
  239.4 381.3 %all-reduce.3.cloned.1.call-start = ((), (), s32[]{:S(2)}) async-start(), calls=%async_computation.2 | async-start | bytes 16613376 | tf_op jit(solution)/shard_map/psum | solution.py:69
Sparse Core Ops, SparseCore 0:
  469.8 150.7 all-reduce.2
where the time goes:
time: 641 us; the launch traced here: 631 us
  waiting for transfers between devices  177 us (28%)
  local copies, waits for them, and re-layouts  175 us (27%)
  blocking collectives  131 us (20%)
  matrix products  96.3 us (15%)
  other arithmetic  24.9 us (4%)
  between operations  14.7 us (2%)
  starting transfers between devices  12.2 us (2%)
    psum x1, waiting for transfers between devices, body(): summed = lax.psum(flat_terms, 'lat')  151 us
    unnamed x1, blocking collectives  131 us
    reshape x1, local copies, waits for them, and re-layouts, body(): table_h = legendre_h.reshape(band_rows, owned_count, MAXM)  51.6 us
    reshape x1, local copies, waits for them, and re-layouts, body(): table_p = legendre_p.reshape(band_rows, owned_count, MAXM)  51.2 us
    dot_general x1, matrix products, body(): jnp.einsum('jqn,jqc->qnc', table_h, right_h, preferred_element_type=jnp.f...  29.6 us
    dot_general x1, matrix products, body(): jnp.einsum('jic,iqt->jqtc', circles, table, precision=lax.Precision.HIGHEST)  26.6 us
    all_to_all x1, waiting for transfers between devices, body(): lax.all_to_all(spectral, 'lon', split_axis=1, concat_axis=3, tiled=True)  25.9 us
    dot_general x1, matrix products, body(): jnp.einsum('jqn,jqc->qnc', table_p, right_p, preferred_element_type=jnp.f...  25.4 us
  transfers between devices with their start and end apart: 3, of which 2 were waited for; matrix products, arithmetic and copies ran while one was open for 20% of the time, Pallas kernels for 0%

commit v1 on v0

v1 whole, which is shorter than its diff:
```python
import functools
import math

import jax
import jax.numpy as jnp
from jax import lax
from jax.experimental import pallas as pl
from jax.experimental.pallas import tpu as pltpu
from jax.sharding import PartitionSpec as P

NLON = 1440
NLAT = 720
MAXM = 720
LEV = 2
DAYS = 8
S = 16
LANES = 128
HALF = 64
VMEM_LIMIT = 56 * 1024 * 1024


def up(value, step):
    return -(-value // step) * step


class Plan:
    def __init__(self, rows, lons, owned, lon_count, lat_count):
        self.rows, self.lons, self.owned = rows, lons, owned
        self.n, self.lat_count = lon_count, lat_count
        self.cols = 2 * S // lon_count
        self.row_pad = up(rows, 8)
        self.stride = up(rows, HALF)
        self.full, self.rem = divmod(lons, LANES)
        assert 0 < self.rem < HALF
        pairs = 2 if self.cols % 2 == 0 else 1
        self.per_chunk = pairs
        self.chunks = self.cols // pairs
        self.blocks = pairs * self.full + 1
        self.depth = lon_count * (self.full * LANES + HALF)
        self.circles = self.cols * self.stride
        self.chunk_circles = pairs * self.stride
        self.share = owned * MAXM // lat_count
        self.first = [self.share * t // MAXM for t in range(lat_count)]
        last = [-(-self.share * (t + 1) // MAXM) for t in range(lat_count)]
        self.cover = max(b - a for a, b in zip(self.first, last))
        parts = 3
        sizes = [self.cover // parts + (1 if i < self.cover % parts else 0) for i in range(parts)]
        self.sizes = [s for s in sizes if s]
        self.starts = [sum(self.sizes[:i]) for i in range(len(self.sizes))]
        self.position_count = [lat_count * s for s in self.sizes]
        self.position_start = [lat_count * s for s in self.starts]
        slots = []
        for start, size in zip(self.starts, self.sizes):
            for t in range(lat_count):
                slots += [self.first[t] + start + i for i in range(size)]
        self.slots = slots
        assert len(slots) <= self.row_pad


def lane_iota(shape):
    return lax.broadcasted_iota(jnp.int32, shape, len(shape) - 1)


def flux_kernel(plan, tile, lev_ref, cos_ref, slot_ref, u_ref, v_ref, z_ref, *refs):
    outs, scratch = refs[:-1], refs[-1]
    me = lax.axis_index("lon")
    level = lev_ref[...]

    def eddy(x):
        out = x
        for a in range(LEV):
            mask = (level == a).astype(jnp.float32)[None]
            mean = jnp.sum(x * mask, axis=1, keepdims=True) * (1.0 / DAYS)
            out = out - mean * mask
        return out

    eddy_z = eddy(z_ref[...])
    for f, ref in enumerate((u_ref, v_ref)):
        flux = eddy(ref[...]) * eddy_z
        for b in range(plan.full):
            part = flux[:, :, b * LANES : (b + 1) * LANES]
            scratch[f, b] = part.reshape(tile * S, LANES)
        part = flux[:, :, plan.full * LANES :]
        scratch[f, plan.full, :, 0 : plan.rem] = part.reshape(tile * S, plan.rem)
    cosine = cos_ref[...]
    lane = lane_iota((tile, LANES))
    per_field = plan.n // 2
    for k in range(plan.n):
        dest = lax.bitwise_xor(me, k)
        field = dest // per_field
        sample = lax.rem(dest, per_field) * plan.cols
        for chunk in range(plan.chunks):
            out = outs[chunk * plan.n + k]
            packed = jnp.zeros((tile, LANES), jnp.float32)
            for c in range(plan.per_chunk):
                rows = pl.ds(sample + chunk * plan.per_chunk + c, tile, stride=S)
                for b in range(plan.full):
                    out[c * plan.full + b] = scratch[field, b, rows, :] * cosine
                tail = jnp.where(lane < plan.rem, scratch[field, plan.full, rows, :] * cosine, 0.0)
                if c:
                    tail = pltpu.roll(tail, HALF * c, 1)
                packed = packed + tail
            if chunk == 0:
                packed = jnp.where(lane == HALF - 1, slot_ref[...], packed)
            out[plan.per_chunk * plan.full] = packed


def flux_call(plan, level, cosine, slots, u, v, z):
    tile = min(48, plan.row_pad)
    field = pl.BlockSpec((tile, S, plan.lons), lambda i: (i, 0, 0))
    column = pl.BlockSpec((tile, 1), lambda i: (i, 0))
    return pl.pallas_call(
        functools.partial(flux_kernel, plan, tile),
        grid=(pl.cdiv(plan.row_pad, tile),),
        in_specs=[pl.BlockSpec((S, 1), lambda i: (0, 0)), column, column, field, field, field],
        out_specs=[pl.BlockSpec((plan.blocks, tile, LANES), lambda i: (0, i, 0))]
        * (plan.chunks * plan.n),
        out_shape=[jax.ShapeDtypeStruct((plan.blocks, plan.row_pad, LANES), jnp.float32)]
        * (plan.chunks * plan.n),
        scratch_shapes=[pltpu.VMEM((2, plan.full + 1, tile * S, LANES), jnp.float32)],
        compiler_params=pltpu.CompilerParams(vmem_limit_bytes=VMEM_LIMIT),
        name="eddy_flux",
    )(level, cosine, slots, u, v, z)


def sincos(x):
    r = x - NLON * jnp.floor(x * (1.0 / NLON) + 0.5)
    q = jnp.floor(r * (4.0 / NLON) + 0.5)
    t = (r - q * (NLON // 4)) * (2.0 * math.pi / NLON)
    t2 = t * t
    s = t * (1.0 + t2 * (-1.0 / 6 + t2 * (1.0 / 120 + t2 * (-1.0 / 5040 + t2 * (1.0 / 362880)))))
    c = 1.0 + t2 * (
        -0.5 + t2 * (1.0 / 24 + t2 * (-1.0 / 720 + t2 * (1.0 / 40320 + t2 * (-1.0 / 3628800))))
    )
    size = jnp.abs(q)
    odd, flip = size == 1.0, size == 2.0
    cosine = jnp.where(odd, -q * s, jnp.where(flip, -c, c))
    sine = jnp.where(odd, q * c, jnp.where(flip, -s, s))
    return cosine, sine


def table_kernel(plan, *refs):
    pieces = refs[: plan.n]
    parts = len(plan.sizes)
    highs, lows = refs[plan.n : plan.n + parts], refs[plan.n + parts : plan.n + 2 * parts]
    held = refs[-1]
    me = lax.axis_index("lon")
    for k in range(plan.n):
        held[k] = pieces[k][0]

    @pl.loop(0, plan.n)
    def _(k):
        for j, count in enumerate(plan.position_count):
            start = plan.position_start[j]
            wave = held[k, start : start + count, HALF - 1 : HALF]
            weight = jnp.where(wave >= 0.0, 1.0 / NLON, 0.0)
            wave = jnp.maximum(wave, 0.0)
            lane = lane_iota((count, LANES))
            source = lax.bitwise_xor(lane, me).astype(jnp.float32) * plan.lons
            turn_cos, turn_sin = sincos(wave * source)
            base = []
            for b in range(plan.full):
                c, s = sincos(wave * (lane + b * LANES).astype(jnp.float32))
                base.append((c * weight, s * weight))
            tail_lane = lane_iota((count, HALF))
            c, s = sincos(wave * (tail_lane + plan.full * LANES).astype(jnp.float32))
            tail_weight = jnp.where(tail_lane < plan.rem, weight, 0.0)
            c, s = c * tail_weight, s * tail_weight

            def put(where, cosine, sine):
                for row, value in ((0, cosine), (count, sine)):
                    high = value.astype(jnp.bfloat16)
                    highs[j][k, row : row + count, where] = high
                    lows[j][k, row : row + count, where] = (
                        value - high.astype(jnp.float32)
                    ).astype(jnp.bfloat16)

            for src in range(plan.n):
                tc, ts = turn_cos[:, src : src + 1], turn_sin[:, src : src + 1]
                for b in range(plan.full):
                    at = (src * plan.full + b) * LANES
                    bc, bs = base[b]
                    put(slice(at, at + LANES), tc * bc - ts * bs, ts * bc + tc * bs)
            for src in range(0, plan.n, 2):
                at = plan.n * plan.full * LANES + src * HALF
                both = []
                for x in (src, src + 1):
                    tc, ts = turn_cos[:, x : x + 1], turn_sin[:, x : x + 1]
                    both.append((tc * c - ts * s, ts * c + tc * s))
                put(
                    slice(at, at + LANES),
                    jnp.concatenate([both[0][0], both[1][0]], axis=1),
                    jnp.concatenate([both[0][1], both[1][1]], axis=1),
                )


def table_call(plan, pieces):
    tail = pl.BlockSpec((1, plan.row_pad, LANES), lambda i: (plan.blocks - 1, 0, 0))
    shapes = [
        jax.ShapeDtypeStruct((plan.n, 2 * count, plan.depth), jnp.bfloat16)
        for count in plan.position_count
    ]
    out = pl.pallas_call(
        functools.partial(table_kernel, plan),
        grid=(1,),
        in_specs=[tail] * plan.n,
        out_specs=[pl.BlockSpec(x.shape, lambda i: (0, 0, 0)) for x in shapes * 2],
        out_shape=shapes * 2,
        scratch_shapes=[pltpu.VMEM((plan.n, plan.row_pad, LANES), jnp.float32)],
        compiler_params=pltpu.CompilerParams(vmem_limit_bytes=VMEM_LIMIT),
        cost_estimate=pl.CostEstimate(flops=10**9, bytes_accessed=10**7, transcendentals=0),
        name="wave_table",
    )(*pieces)
    parts = len(plan.sizes)
    return list(zip(out[:parts], out[parts:]))


def split_kernel(plan, *refs):
    pieces, (high, low) = refs[: plan.n], refs[plan.n :]

    def put(rows, lanes, value):
        top = value.astype(jnp.bfloat16)
        high[rows, lanes] = top
        low[rows, lanes] = (value - top.astype(jnp.float32)).astype(jnp.bfloat16)

    base = plan.n * plan.full * LANES
    for c in range(plan.per_chunk):
        rows = slice(c * plan.stride, c * plan.stride + plan.row_pad)
        for k in range(plan.n):
            for b in range(plan.full):
                at = (k * plan.full + b) * LANES
                put(rows, slice(at, at + LANES), pieces[k][c * plan.full + b])
        for k in range(0, plan.n, 2):
            at = base + k * HALF
            first, second = pieces[k][plan.blocks - 1], pieces[k + 1][plan.blocks - 1]
            lane = lane_iota(first.shape)
            if c:
                first = pltpu.roll(first, LANES - HALF * c, 1)
            else:
                second = pltpu.roll(second, HALF, 1)
            put(rows, slice(at, at + LANES), jnp.where(lane < HALF, first, second))


def split_call(plan, pieces):
    shape = jax.ShapeDtypeStruct((plan.chunk_circles, plan.depth), jnp.bfloat16)
    return pl.pallas_call(
        functools.partial(split_kernel, plan),
        out_shape=[shape, shape],
        compiler_params=pltpu.CompilerParams(vmem_limit_bytes=VMEM_LIMIT),
        cost_estimate=pl.CostEstimate(flops=10**8, bytes_accessed=10**7, transcendentals=0),
        name="split_circles",
    )(*pieces)


def dft_kernel(plan, th_ref, tl_ref, *refs):
    outs = refs[2 * plan.chunks :]
    count = th_ref.shape[1]
    shape = (plan.n * count, plan.depth)
    th, tl = th_ref[...].reshape(shape), tl_ref[...].reshape(shape)
    for chunk in range(plan.chunks):
        fh, fl = refs[2 * chunk][...], refs[2 * chunk + 1][...]
        dims = (((1,), (1,)), ((), ()))
        dot = functools.partial(
            lax.dot_general, dimension_numbers=dims, preferred_element_type=jnp.float32
        )
        total = dot(th, fh) + (dot(th, fl) + dot(tl, fh))
        lanes = slice(chunk * plan.chunk_circles, (chunk + 1) * plan.chunk_circles)
        for k in range(plan.n):
            outs[k][:, lanes] = total[k * count : (k + 1) * count]


def dft_call(plan, table, circles):
    count = table[0].shape[1]
    flops = 6 * plan.n * count * plan.depth * plan.circles
    return pl.pallas_call(
        functools.partial(dft_kernel, plan),
        out_shape=[jax.ShapeDtypeStruct((count, plan.circles), jnp.float32)] * plan.n,
        compiler_params=pltpu.CompilerParams(vmem_limit_bytes=VMEM_LIMIT),
        cost_estimate=pl.CostEstimate(flops=flops, bytes_accessed=10**7, transcendentals=0),
        name="dft",
    )(*table, *[x for pair in circles for x in pair])


def legendre_kernel(plan, part, wide, buffers, wave_ref, scale_ref, *refs):
    pieces = refs[: plan.n]
    tables = refs[plan.n : plan.n + 2]
    edges = refs[plan.n + 2 : plan.n + 4]
    out_ref, right, held, sems = refs[plan.n + 4 :]
    size, start = plan.sizes[part], plan.starts[part]
    count, offset = plan.position_count[part], plan.position_start[part]
    total = plan.owned * MAXM
    me = lax.axis_index("lon")
    inner = wide - LANES

    def place(p):
        t = p // size
        slot = (plan.share * t) // MAXM + start + lax.rem(p, size)
        column = jnp.minimum(slot, plan.owned - 1) * MAXM
        shift = lax.rem(column, LANES)
        return column - shift, shift

    def copies(p, act):
        base, _ = place(p)
        buffer = lax.rem(p, buffers)
        base = pl.multiple_of(base, LANES)
        for f in range(2):
            sem = sems.at[buffer, f]
            act(
                pltpu.make_async_copy(
                    tables[f].at[:, pl.ds(base, inner)],
                    held.at[buffer, f, :, pl.ds(0, inner)],
                    sem,
                )
            )
            last = pl.multiple_of(base + inner, LANES)
            fits = base + wide <= total

            @pl.when(fits)
            def _():
                act(
                    pltpu.make_async_copy(
                        tables[f].at[:, pl.ds(last, LANES)],
                        held.at[buffer, f, :, pl.ds(inner, LANES)],
                        sems.at[buffer, 2 + f],
                    )
                )

            @pl.when(jnp.logical_not(fits))
            def _():
                act(
                    pltpu.make_async_copy(
                        edges[f],
                        held.at[buffer, f, :, pl.ds(inner, LANES)],
                        sems.at[buffer, 2 + f],
                    )
                )

    for p in range(min(buffers - 1, count)):
        copies(jnp.int32(p), lambda c: c.start())

    per_field = plan.n // 2
    scale = scale_ref[...]
    for k in range(plan.n):
        source = lax.bitwise_xor(me, k)
        field = source // per_field
        sample = lax.rem(source, per_field) * plan.cols
        for cs in range(2):
            factor = jnp.where(field == 0, scale, -1.0 if cs == 0 else 1.0)
            imaginary = field if cs else 1 - field
            for c in range(plan.cols):
                value = pieces[k][cs * count : (cs + 1) * count, c * plan.stride : (c + 1) * plan.stride]
                value = value * factor
                rows = pl.ds(imaginary * S + sample + c, count, stride=2 * S)
                for b in range(plan.stride // LANES):
                    right[field, b, rows, :] = value[:, b * LANES : (b + 1) * LANES]
                if plan.stride % LANES:
                    b = plan.stride // LANES
                    right[field, b, rows, 0:HALF] = value[:, b * LANES :]

    blocks = pl.cdiv(plan.stride, LANES)

    @pl.loop(0, count)
    def _(p):
        @pl.when(p + buffers - 1 < count)
        def _():
            copies(p + buffers - 1, lambda c: c.start())

        copies(p, lambda c: c.wait())
        buffer = lax.rem(p, buffers)
        _, shift = place(p)
        sums = None
        rows = pl.ds(pl.multiple_of(p * 2 * S, 2 * S), 2 * S)
        for f in range(2):
            left = [right[f, b, rows, :] for b in range(blocks)]
            left = jnp.concatenate(left, axis=1)[:, : plan.rows].astype(jnp.bfloat16)
            term = jnp.dot(left, held[buffer, f], preferred_element_type=jnp.float32)
            sums = term if sums is None else sums + term
        sums = pltpu.roll(sums, lax.rem(wide - shift, wide), 1)[:, :inner]
        degree = lane_iota((2 * S, inner))
        wave = wave_ref[offset + p]
        keep = (degree >= wave) & (degree < MAXM) & (wave >= 0)
        out_ref[p] = jnp.where(keep, sums, 0.0)


def legendre_call(plan, part, wave, scale, pieces, tables, edges):
    wide = up(MAXM, LANES) + LANES
    buffers = 4
    count = plan.position_count[part]
    vmem = pl.BlockSpec(memory_space=pltpu.VMEM)
    hbm = pl.BlockSpec(memory_space=pl.ANY)
    blocks = pl.cdiv(plan.stride, LANES)
    return pl.pallas_call(
        functools.partial(legendre_kernel, plan, part, wide, buffers),
        in_specs=[pl.BlockSpec(memory_space=pltpu.SMEM), vmem]
        + [vmem] * plan.n
        + [hbm, hbm]
        + [hbm, hbm],
        out_specs=vmem,
        out_shape=jax.ShapeDtypeStruct((count, 2 * S, wide - LANES), jnp.float32),
        scratch_shapes=[
            pltpu.VMEM((2, blocks, count * 2 * S, LANES), jnp.float32),
            pltpu.VMEM((buffers, 2, plan.rows, wide), jnp.bfloat16),
            pltpu.SemaphoreType.DMA((buffers, 4)),
        ],
        compiler_params=pltpu.CompilerParams(vmem_limit_bytes=VMEM_LIMIT),
        cost_estimate=pl.CostEstimate(
            flops=4 * count * 2 * S * plan.rows * wide,
            bytes_accessed=4 * count * plan.rows * wide,
            transcendentals=0,
        ),
        name="legendre",
    )(wave, scale, *pieces, *tables, *edges)


def exchange(plan, pieces):
    order = sorted(range(1, plan.n), key=lambda k: -k)
    got = {0: pieces[0]}
    for k in order:
        got[k] = lax.ppermute(pieces[k], "lon", [(i, i ^ k) for i in range(plan.n)])
    return [got[k] for k in range(plan.n)]


def body(wind_u, wind_v, vorticity, sample_level, slot_wavenumber, legendre_p, legendre_h):
    rows, lons = wind_u.shape[0], wind_u.shape[1]
    lon_count, lat_count = lax.axis_size("lon"), lax.axis_size("lat")
    plan = Plan(rows, lons, slot_wavenumber.shape[0], lon_count, lat_count)
    row_index = lax.axis_index("lat") * rows + jnp.arange(plan.row_pad, dtype=jnp.int32)
    latitude = (row_index.astype(jnp.float32) + 0.5) * (math.pi / NLAT) - 0.5 * math.pi
    cosine = jnp.cos(latitude)[:, None]
    wave = jnp.concatenate([slot_wavenumber, jnp.full((1,), -1, jnp.int32)])
    picks = [min(s, plan.owned) for s in plan.slots]
    wave = wave[jnp.array(picks, jnp.int32)]
    column = jnp.concatenate(
        [wave.astype(jnp.float32), jnp.full((plan.row_pad - len(picks),), -1.0, jnp.float32)]
    )[:, None]
    fields = [jnp.transpose(x, (0, 2, 1)) for x in (wind_u, wind_v, vorticity)]
    sent = flux_call(plan, sample_level[:, None], cosine, column, *fields)
    n = plan.n
    got = [exchange(plan, sent[i * n : (i + 1) * n]) for i in range(plan.chunks)]
    tables = table_call(plan, got[0])
    circles = [split_call(plan, pieces) for pieces in got]
    scale = (jnp.maximum(wave, 0).astype(jnp.float32) / MAXM)[:, None]
    edge_start = plan.owned * MAXM // LANES * LANES
    edges = []
    for table in (legendre_p, legendre_h):
        edge = table[:, edge_start:]
        edges.append(jnp.pad(edge, ((0, 0), (0, LANES - edge.shape[1]))))
    onehot = (sample_level[:, None] == jnp.arange(LEV, dtype=jnp.int32)[None, :]).astype(
        jnp.float32
    )
    powers = []
    for part, size in enumerate(plan.sizes):
        coeffs = exchange(plan, dft_call(plan, tables[part], circles))
        first, count = plan.position_start[part], plan.position_count[part]
        sums = legendre_call(
            plan, part, wave, scale[first : first + count], coeffs, (legendre_p, legendre_h), edges
        )
        mine = lax.psum_scatter(sums, "lat", scatter_dimension=0, tiled=True)
        power = mine[:, :S] ** 2 + mine[:, S:] ** 2
        powers.append(
            jnp.einsum("isx,sl->lix", power, onehot, precision=lax.Precision.HIGHEST) / DAYS
        )
    spectra = jnp.concatenate(powers, axis=1)[:, :, :MAXM].reshape(LEV, plan.cover * MAXM)
    begin = jnp.array([plan.share * t - f * MAXM for t, f in enumerate(plan.first)], jnp.int32)
    return lax.dynamic_slice_in_dim(spectra, begin[lax.axis_index("lat")], plan.share, 1)


def solution(mesh):
    placed = (
        P("lat", "lon", None),
        P("lat", "lon", None),
        P("lat", "lon", None),
        P(),
        P("lon"),
        P("lat", "lon"),
        P("lat", "lon"),
    )
    return jax.shard_map(
        body, mesh=mesh, in_specs=placed, out_specs=P(None, ("lon", "lat")), check_vma=False
    )
```

time: 641 us -> 380 us (0.59); the launches traced: 631 us -> 379 us
  local copies, waits for them, and re-layouts: 175 us -> 12.4 us
  blocking collectives: 131 us -> 0 us
  Pallas kernels: 0 us -> 112 us
  matrix products: 96.3 us -> 4.18 us
  starting transfers between devices: 12.2 us -> 65.7 us
  other arithmetic: 24.9 us -> 2.43 us
  waiting for transfers between devices: 177 us -> 166 us
    psum x1 -> x0, waiting for transfers between devices: 151 us -> none  [body(): summed = lax.psum(flat_terms, 'lat')]
    unnamed x1 -> x0, blocking collectives: 131 us -> none
    ppermute x0 -> x35, waiting for transfers between devices: none -> 131 us  [exchange(): got[k] = lax.ppermute(pieces[k], 'lon', [(i, i ^ k) for i in range(plan.n)])]
    pallas_call x0 -> x10, Pallas kernels: none -> 112 us  [the longest x3 53.2 us: legendre_call(): pl.pallas_call(functools.partial(legendre_kernel, plan, part, wide, buffe...]
    reshape x3 -> x1, local copies, waits for them, and re-layouts: 113 us -> 0.2 us  [body(): jnp.concatenate(powers, axis=1)[:, :, :MAXM].reshape(LEV, plan.cover * MAXM)]
    dot_general x10 -> x3, matrix products: 96.3 us -> 4.18 us  [body(): jnp.einsum('isx,sl->lix', power, onehot, precision=lax.Precision.HIGHEST)]
    ppermute x0 -> x35, starting transfers between devices: none -> 65.4 us  [exchange(): got[k] = lax.ppermute(pieces[k], 'lon', [(i, i ^ k) for i in range(plan.n)])]
    all_to_all x5 -> x0, local copies, waits for them, and re-layouts: 38 us -> none  [the longest x3 22.7 us: body(): lax.all_to_all(spectral, 'lon', split_axis=1, concat_axis=3, tiled=True)]
  transfers between devices with their start and end apart: 3 -> 38, of which waited for: 2 -> 17; matrix products, arithmetic and copies ran while one was open for 20% -> 2% of each run, Pallas kernels for 0% -> 19%
where the time goes in v1:
time: 380 us; the launch traced here: 379 us
  waiting for transfers between devices  166 us (44%)
  Pallas kernels  112 us (29%)
  starting transfers between devices  65.7 us (17%)
  between operations  15.5 us (4%)
  local copies, waits for them, and re-layouts  12.4 us (3%)
  matrix products  4.18 us (1%)
    ppermute x35, waiting for transfers between devices, exchange(): got[k] = lax.ppermute(pieces[k], 'lon', [(i, i ^ k) for i in range(plan.n)])  131 us
    ppermute x35, starting transfers between devices, exchange(): got[k] = lax.ppermute(pieces[k], 'lon', [(i, i ^ k) for i in range(plan.n)])  65.4 us
    pallas_call x3, Pallas kernels, legendre_call(): pl.pallas_call(functools.partial(legendre_kernel, plan, part, wide, buffe...  53.2 us
    reduce_scatter x3, waiting for transfers between devices, body(): mine = lax.psum_scatter(sums, 'lat', scatter_dimension=0, tiled=True)  35.3 us
    pallas_call x3, Pallas kernels, dft_call(): pl.pallas_call(functools.partial(dft_kernel, plan), out_shape=[jax.ShapeD...  27.2 us
    pallas_call x1, Pallas kernels, flux_call(): pl.pallas_call(functools.partial(flux_kernel, plan, tile), grid=(pl.cdiv(...  13.5 us
    pallas_call x1, Pallas kernels, table_call(): pl.pallas_call(functools.partial(table_kernel, plan), grid=(1,), in_specs...  11.9 us
  transfers between devices with their start and end apart: 38, of which 17 were waited for; matrix products, arithmetic and copies ran while one was open for 2% of the time, Pallas kernels for 19%

profile of v1, /device:TPU:0, one launch (start us, length us, event | category | flops | bytes accessed | tf_op | source)
XLA Modules:
  0.0 378.5 jit_solution(11260844738085195130)
XLA Ops:
  12.3 13.5 %eddy_flux.1 = (f32[3,184,128]{2,1,0:T(8,128)}, f32[3,184,128]{2,1,0:T(8,128)}, f32[3,184,128]{2,1,0:T(8,128)}, f32[3,184,128]{2,1,0:T(8,128)}, f32[3,184,128]{2...) custom-call(s32[16,1]{1,0:T(8,128)} %copy.21.lev_ref, ...), custom_call_target="tpu_custom_call" | custom-call | tf_op jit(solution)/shard_map/eddy_flux/pallas_call | solution.py:112
  25.8 3.0 collective-permute-start
  30.4 3.0 collective-permute-start.3
  35.8 3.8 %collective-permute-start.5 = (f32[3,184,128]{2,1,0:T(8,128)}, f32[3,184,128]{2,1,0:T(8,128)S(1)}, u32[]{:S(2)}, u32[]{:S(2)}) collective-permute-start(f32[3,184,128]{2,1,0:T(8,128)} %get-tuple-element.61), channel_id=1, source_target_pairs={{0,24},{4,28},{8,16},{12,20},{16,8},{20,12},{24,0},{28,4},{1,25},{... | collective-permute-start | bytes 847880 | tf_op jit(solution)/shard_map/ppermute | solution.py:419
  39.6 10.3 %collective-permute-done.1.refs_2_ = f32[3,184,128]{2,1,0:T(8,128)S(1)} collective-permute-done((f32[3,184,128]{2,1,0:T(8,128)}, f32[3,184,128]{2,1,0:T(8,128)S(1)}, u32[]{:S(2)}, u32[]{:S(2)}) %collective-permute-start.1) | collective-permute-done | bytes 282656 | tf_op jit(solution)/shard_map/ppermute | solution.py:419
  54.7 3.6 collective-permute-start.11
  58.3 26.6 %collective-permute-done.4.refs_5_ = f32[3,184,128]{2,1,0:T(8,128)S(1)} collective-permute-done((f32[3,184,128]{2,1,0:T(8,128)}, f32[3,184,128]{2,1,0:T(8,128)S(1)}, u32[]{:S(2)}, u32[]{:S(2)}) %collective-permute-start.4) | collective-permute-done | bytes 282656 | tf_op jit(solution)/shard_map/ppermute | solution.py:419
  85.0 3.6 collective-permute-start.12
  90.3 23.7 %collective-permute-done.10.refs_4_ = f32[3,184,128]{2,1,0:T(8,128)S(1)} collective-permute-done((f32[3,184,128]{2,1,0:T(8,128)}, f32[3,184,128]{2,1,0:T(8,128)S(1)}, u32[]{:S(2)}, u32[]{:S(2)}) %collective-permute-start.10) | collective-permute-done | bytes 282656 | tf_op jit(solution)/shard_map/ppermute | solution.py:419
  115.2 6.2 %collective-permute-done.11.refs_5_ = f32[3,184,128]{2,1,0:T(8,128)S(1)} collective-permute-done((f32[3,184,128]{2,1,0:T(8,128)}, f32[3,184,128]{2,1,0:T(8,128)S(1)}, u32[]{:S(2)}, u32[]{:S(2)}) %collective-permute-start.11) | collective-permute-done | bytes 282656 | tf_op jit(solution)/shard_map/ppermute | solution.py:419
  123.5 3.3 split_circles.2
  126.9 11.9 %wave_table.1 = (bf16[8,64,1536]{2,1,0:T(8,128)(2,1)}, bf16[8,64,1536]{2,1,0:T(8,128)(2,1)}, bf16[8,56,1536]{2,1,0:T(8,128)(2,1)}, bf16[8,64,1536]{2,1,0:T(8,128...) custom-call(f32[3,184,128]{2,1,0:T(8,128)} %get-tuple-element.55.refs_0_, f32[3,184,128]{2,1,0:T(8,128)} %copy-done, ...), custom_call_target="tpu_custom_call" | custom-call | flops 1000000000 | bytes 10000000 | tf_op jit(solution)/shard_map/wave_table/pallas_call | solution.py:203
  139.8 3.3 split_circles.3
  143.1 8.6 %dft.5 = (f32[56,768]{1,0:T(8,128)}, f32[56,768]{1,0:T(8,128)}, f32[56,768]{1,0:T(8,128)}, f32[56,768]{1,0:T(8,128)}, f32[56,768]{1,0:T(8,128)}, /*index=5*/f32[...) custom-call(bf16[8,56,1536]{2,1,0:T(8,128)(2,1)} %get-tuple-element.95.th_ref, ...), custom_call_target="tpu_custom_call" | custom-call | flops 3170893824 | bytes 10000000 | tf_op jit(solution)/shard_map/dft/pallas_call | solution.py:275
  155.2 3.2 collective-permute-start.31
  164.6 12.0 %collective-permute-done.31.refs_4_ = f32[56,768]{1,0:T(8,128)S(1)} collective-permute-done((f32[56,768]{1,0:T(8,128)}, f32[56,768]{1,0:T(8,128)S(1)}, u32[]{:S(2)}, u32[]{:S(2)}) %collective-permute-start.31) | collective-permute-done | bytes 172064 | tf_op jit(solution)/shard_map/ppermute | solution.py:419
  176.7 4.1 %collective-permute-done.32.refs_5_ = f32[56,768]{1,0:T(8,128)S(1)} collective-permute-done((f32[56,768]{1,0:T(8,128)}, f32[56,768]{1,0:T(8,128)S(1)}, u32[]{:S(2)}, u32[]{:S(2)}) %collective-permute-start.32) | collective-permute-done | bytes 172064 | tf_op jit(solution)/shard_map/ppermute | solution.py:419
  181.6 16.8 %legendre.5 = f32[28,32,768]{2,1,0:T(8,128)} custom-call(s32[92]{0:T(128)} %copy-done.35, f32[28,1]{1,0:T(8,128)} %copy.25.scale_ref, f32[56,768]{1,0:T(8,128)} %get-tuple-element.97.refs_0_, f32[56,768]{1,0:T(8,128)} %copy-done.28, f32[56,768]{1,0:T(8,128)} %copy-done.29, f32[56,768]{1,0:T(8,128)} %copy-done.30, f32[56,768]{1,0:T(8,128)} %copy-done.31, ...), custom_call_target="tpu_custom_call" | custom-call | flops 578027520 | bytes 18063360 | tf_op jit(solution)/shard_map/legendre/pallas_call | solution.py:392
  198.6 9.3 %dft.3 = (f32[64,768]{1,0:T(8,128)}, f32[64,768]{1,0:T(8,128)}, f32[64,768]{1,0:T(8,128)}, f32[64,768]{1,0:T(8,128)}, f32[64,768]{1,0:T(8,128)}, /*index=5*/f32[...) custom-call(bf16[8,64,1536]{2,1,0:T(8,128)(2,1)} %get-tuple-element.63.th_ref, ...), custom_call_target="tpu_custom_call" | custom-call | flops 3623878656 | bytes 10000000 | tf_op jit(solution)/shard_map/dft/pallas_call | solution.py:275
  209.0 5.5 %collective-permute-start.15 = (f32[64,768]{1,0:T(8,128)}, f32[64,768]{1,0:T(8,128)S(1)}, u32[]{:S(2)}, u32[]{:S(2)}) collective-permute-start(f32[64,768]{1,0:T(8,128)} %get-tuple-element.79), channel_id=1, source_target_pairs={{0,8},{4,12},{8,0},{12,4},{16,24},{20,28},{24,16},{28,20},{1,9},{5... | collective-permute-start | bytes 589832 | tf_op jit(solution)/shard_map/ppermute | solution.py:419
  219.8 4.9 %collective-permute-done.15.refs_2_ = f32[64,768]{1,0:T(8,128)S(1)} collective-permute-done((f32[64,768]{1,0:T(8,128)}, f32[64,768]{1,0:T(8,128)S(1)}, u32[]{:S(2)}, u32[]{:S(2)}) %collective-permute-start.15) | collective-permute-done | bytes 196640 | tf_op jit(solution)/shard_map/ppermute | solution.py:419
  226.1 2.8 collective-permute-done.16.refs_3_
  228.9 10.6 %collective-permute-done.17.refs_4_ = f32[64,768]{1,0:T(8,128)S(1)} collective-permute-done((f32[64,768]{1,0:T(8,128)}, f32[64,768]{1,0:T(8,128)S(1)}, u32[]{:S(2)}, u32[]{:S(2)}) %collective-permute-start.17) | collective-permute-done | bytes 196640 | tf_op jit(solution)/shard_map/ppermute | solution.py:419
  239.5 4.5 %collective-permute-done.18.refs_5_ = f32[64,768]{1,0:T(8,128)S(1)} collective-permute-done((f32[64,768]{1,0:T(8,128)}, f32[64,768]{1,0:T(8,128)S(1)}, u32[]{:S(2)}, u32[]{:S(2)}) %collective-permute-start.18) | collective-permute-done | bytes 196640 | tf_op jit(solution)/shard_map/ppermute | solution.py:419
  244.8 18.2 %legendre.3 = f32[32,32,768]{2,1,0:T(8,128)} custom-call(s32[92]{0:T(128)} %copy-done.35, f32[32,1]{1,0:T(8,128)} %copy.23.scale_ref, f32[64,768]{1,0:T(8,128)} %get-tuple-element.77.refs_0_, f32[64,768]{1,0:T(8,128)} %copy-done.14, f32[64,768]{1,0:T(8,128)} %copy-done.16, f32[64,768]{1,0:T(8,128)} %copy-done.18, f32[64,768]{1,0:T(8,128)} %copy-done.20, ...), custom_call_target="tpu_custom_call" | custom-call | flops 660602880 | bytes 20643840 | tf_op jit(solution)/shard_map/legendre/pallas_call | solution.py:392
  263.1 9.3 %dft.4 = (f32[64,768]{1,0:T(8,128)}, f32[64,768]{1,0:T(8,128)}, f32[64,768]{1,0:T(8,128)}, f32[64,768]{1,0:T(8,128)}, f32[64,768]{1,0:T(8,128)}, /*index=5*/f32[...) custom-call(bf16[8,64,1536]{2,1,0:T(8,128)(2,1)} %get-tuple-element.85.th_ref, ...), custom_call_target="tpu_custom_call" | custom-call | flops 3623878656 | bytes 10000000 | tf_op jit(solution)/shard_map/dft/pallas_call | solution.py:275
  273.6 5.6 %collective-permute-start.22 = (f32[64,768]{1,0:T(8,128)}, f32[64,768]{1,0:T(8,128)S(1)}, u32[]{:S(2)}, u32[]{:S(2)}) collective-permute-start(f32[64,768]{1,0:T(8,128)} %get-tuple-element.89), channel_id=1, source_target_pairs={{0,8},{4,12},{8,0},{12,4},{16,24},{20,28},{24,16},{28,20},{1,9},{5... | collective-permute-start | bytes 589832 | tf_op jit(solution)/shard_map/ppermute | solution.py:419
  285.7 3.3 collective-permute-done.22.refs_2_
  294.0 10.8 %collective-permute-done.24.refs_4_ = f32[64,768]{1,0:T(8,128)S(1)} collective-permute-done((f32[64,768]{1,0:T(8,128)}, f32[64,768]{1,0:T(8,128)S(1)}, u32[]{:S(2)}, u32[]{:S(2)}) %collective-permute-start.24) | collective-permute-done | bytes 196640 | tf_op jit(solution)/shard_map/ppermute | solution.py:419
  304.8 4.2 %collective-permute-done.25.refs_5_ = f32[64,768]{1,0:T(8,128)S(1)} collective-permute-done((f32[64,768]{1,0:T(8,128)}, f32[64,768]{1,0:T(8,128)S(1)}, u32[]{:S(2)}, u32[]{:S(2)}) %collective-permute-start.25) | collective-permute-done | bytes 196640 | tf_op jit(solution)/shard_map/ppermute | solution.py:419
  309.8 18.2 %legendre.4 = f32[32,32,768]{2,1,0:T(8,128)} custom-call(s32[92]{0:T(128)} %copy-done.35, f32[32,1]{1,0:T(8,128)} %copy.24.scale_ref, f32[64,768]{1,0:T(8,128)} %get-tuple-element.87.refs_0_, f32[64,768]{1,0:T(8,128)} %copy-done.15, f32[64,768]{1,0:T(8,128)} %copy-done.17, f32[64,768]{1,0:T(8,128)} %copy-done.19, f32[64,768]{1,0:T(8,128)} %copy-done.21, ...), custom_call_target="tpu_custom_call" | custom-call | flops 660602880 | bytes 20643840 | tf_op jit(solution)/shard_map/legendre/pallas_call | solution.py:392
  334.1 35.3 %reduce-scatter.6.cloned.1.call-done = f32[8,32,768]{2,1,0:T(8,128)} async-done(((f32[32,32,768]{2,1,0:T(8,128)}), f32[8,32,768]{2,1,0:T(8,128)}) %reduce-scatter.6.cloned.1.call-update) | async-done | bytes 786448 | tf_op jit(solution)/shard_map/reduce_scatter | solution.py:458
  (161 shorter events, 59.9 us)
Async XLA Ops:
  6.5 324.8 %reduce-scatter.8.cloned.1.call-start = ((), (), s32[]{:S(2)}) async-start(), calls=%async_computation.5 | async-start | bytes 3440640 | tf_op jit(solution)/shard_map/reduce_scatter | solution.py:458
  28.8 21.0 %collective-permute-start.1 = (f32[3,184,128]{2,1,0:T(8,128)}, f32[3,184,128]{2,1,0:T(8,128)S(1)}, u32[]{:S(2)}, u32[]{:S(2)}) collective-permute-start(f32[3,184,128]{2,1,0:T(8,128)} %get-tuple-element.57), channel_id=1, source_target_pairs={{0,8},{4,12},{8,0},{12,4},{16,24},{20,28},{24,16},{28,20},{1,9},{5... | collective-permute-start | bytes 847880 | tf_op jit(solution)/shard_map/ppermute | solution.py:419
  30.4 23.2 %collective-permute-start.2 = (f32[3,184,128]{2,1,0:T(8,128)}, f32[3,184,128]{2,1,0:T(8,128)S(1)}, u32[]{:S(2)}, u32[]{:S(2)}) collective-permute-start(f32[3,184,128]{2,1,0:T(8,128)} %get-tuple-element.58), channel_id=1, source_target_pairs={{0,12},{4,8},{8,4},{12,0},{16,28},{20,24},{24,20},{28,16},{1,13},{... | collective-permute-start | bytes 847880 | tf_op jit(solution)/shard_map/ppermute | solution.py:419
  30.4 24.3 %collective-permute-start.3 = (f32[3,184,128]{2,1,0:T(8,128)}, f32[3,184,128]{2,1,0:T(8,128)S(1)}, u32[]{:S(2)}, u32[]{:S(2)}) collective-permute-start(f32[3,184,128]{2,1,0:T(8,128)} %get-tuple-element.59), channel_id=1, source_target_pairs={{0,16},{4,20},{8,24},{12,28},{16,0},{20,4},{24,8},{28,12},{1,17},{... | collective-permute-start | bytes 847880 | tf_op jit(solution)/shard_map/ppermute | solution.py:419
  33.4 51.6 %collective-permute-start.4 = (f32[3,184,128]{2,1,0:T(8,128)}, f32[3,184,128]{2,1,0:T(8,128)S(1)}, u32[]{:S(2)}, u32[]{:S(2)}) collective-permute-start(f32[3,184,128]{2,1,0:T(8,128)} %get-tuple-element.60), channel_id=1, source_target_pairs={{0,20},{4,16},{8,28},{12,24},{16,4},{20,0},{24,12},{28,8},{1,21},{... | collective-permute-start | bytes 847880 | tf_op jit(solution)/shard_map/ppermute | solution.py:419
  35.8 52.8 %collective-permute-start.5 = (f32[3,184,128]{2,1,0:T(8,128)}, f32[3,184,128]{2,1,0:T(8,128)S(1)}, u32[]{:S(2)}, u32[]{:S(2)}) collective-permute-start(f32[3,184,128]{2,1,0:T(8,128)} %get-tuple-element.61), channel_id=1, source_target_pairs={{0,24},{4,28},{8,16},{12,20},{16,8},{20,12},{24,0},{28,4},{1,25},{... | collective-permute-start | bytes 847880 | tf_op jit(solution)/shard_map/ppermute | solution.py:419
  49.9 38.7 %collective-permute-start.6 = (f32[3,184,128]{2,1,0:T(8,128)}, f32[3,184,128]{2,1,0:T(8,128)S(1)}, u32[]{:S(2)}, u32[]{:S(2)}) collective-permute-start(f32[3,184,128]{2,1,0:T(8,128)} %get-tuple-element.62), channel_id=1, source_target_pairs={{0,28},{4,24},{8,20},{12,16},{16,12},{20,8},{24,4},{28,0},{1,29},{... | collective-permute-start | bytes 847880 | tf_op jit(solution)/shard_map/ppermute | solution.py:419
  53.6 60.4 %collective-permute-start.10 = (f32[3,184,128]{2,1,0:T(8,128)}, f32[3,184,128]{2,1,0:T(8,128)S(1)}, u32[]{:S(2)}, u32[]{:S(2)}) collective-permute-start(f32[3,184,128]{2,1,0:T(8,128)} %get-tuple-element.71), channel_id=1, source_target_pairs={{0,16},{4,20},{8,24},{12,28},{16,0},{20,4},{24,8},{28,12},{1,17},{... | collective-permute-start | bytes 847880 | tf_op jit(solution)/shard_map/ppermute | solution.py:419
  54.7 66.6 %collective-permute-start.11 = (f32[3,184,128]{2,1,0:T(8,128)}, f32[3,184,128]{2,1,0:T(8,128)S(1)}, u32[]{:S(2)}, u32[]{:S(2)}) collective-permute-start(f32[3,184,128]{2,1,0:T(8,128)} %get-tuple-element.72), channel_id=1, source_target_pairs={{0,20},{4,16},{8,28},{12,24},{16,4},{20,0},{24,12},{28,8},{1,21},{... | collective-permute-start | bytes 847880 | tf_op jit(solution)/shard_map/ppermute | solution.py:419
  85.0 53.8 %collective-permute-start.12 = (f32[3,184,128]{2,1,0:T(8,128)}, f32[3,184,128]{2,1,0:T(8,128)S(1)}, u32[]{:S(2)}, u32[]{:S(2)}) collective-permute-start(f32[3,184,128]{2,1,0:T(8,128)} %get-tuple-element.73), channel_id=1, source_target_pairs={{0,24},{4,28},{8,16},{12,20},{16,8},{20,12},{24,0},{28,4},{1,25},{... | collective-permute-start | bytes 847880 | tf_op jit(solution)/shard_map/ppermute | solution.py:419
  88.6 50.2 %collective-permute-start.13 = (f32[3,184,128]{2,1,0:T(8,128)}, f32[3,184,128]{2,1,0:T(8,128)S(1)}, u32[]{:S(2)}, u32[]{:S(2)}) collective-permute-start(f32[3,184,128]{2,1,0:T(8,128)} %get-tuple-element.74), channel_id=1, source_target_pairs={{0,28},{4,24},{8,20},{12,16},{16,12},{20,8},{24,4},{28,0},{1,29},{... | collective-permute-start | bytes 847880 | tf_op jit(solution)/shard_map/ppermute | solution.py:419
  88.6 50.2 %collective-permute-start.7 = (f32[3,184,128]{2,1,0:T(8,128)}, f32[3,184,128]{2,1,0:T(8,128)S(1)}, u32[]{:S(2)}, u32[]{:S(2)}) collective-permute-start(f32[3,184,128]{2,1,0:T(8,128)} %get-tuple-element.68), channel_id=1, source_target_pairs={{0,4},{4,0},{8,12},{12,8},{16,20},{20,16},{24,28},{28,24},{1,5},{5... | collective-permute-start | bytes 847880 | tf_op jit(solution)/shard_map/ppermute | solution.py:419
  114.0 24.8 %collective-permute-start.8 = (f32[3,184,128]{2,1,0:T(8,128)}, f32[3,184,128]{2,1,0:T(8,128)S(1)}, u32[]{:S(2)}, u32[]{:S(2)}) collective-permute-start(f32[3,184,128]{2,1,0:T(8,128)} %get-tuple-element.69), channel_id=1, source_target_pairs={{0,8},{4,12},{8,0},{12,4},{16,24},{20,28},{24,16},{28,20},{1,9},{5... | collective-permute-start | bytes 847880 | tf_op jit(solution)/shard_map/ppermute | solution.py:419
  121.3 17.5 %collective-permute-start.9 = (f32[3,184,128]{2,1,0:T(8,128)}, f32[3,184,128]{2,1,0:T(8,128)S(1)}, u32[]{:S(2)}, u32[]{:S(2)}) collective-permute-start(f32[3,184,128]{2,1,0:T(8,128)} %get-tuple-element.70), channel_id=1, source_target_pairs={{0,12},{4,8},{8,4},{12,0},{16,28},{20,24},{24,20},{28,16},{1,13},{... | collective-permute-start | bytes 847880 | tf_op jit(solution)/shard_map/ppermute | solution.py:419
  155.2 21.5 %collective-permute-start.31 = (f32[56,768]{1,0:T(8,128)}, f32[56,768]{1,0:T(8,128)S(1)}, u32[]{:S(2)}, u32[]{:S(2)}) collective-permute-start(f32[56,768]{1,0:T(8,128)} %get-tuple-element.101), channel_id=1, source_target_pairs={{0,16},{4,20},{8,24},{12,28},{16,0},{20,4},{24,8},{28,12},{1,17},{... | collective-permute-start | bytes 516104 | tf_op jit(solution)/shard_map/ppermute | solution.py:419
  158.4 22.4 %collective-permute-start.32 = (f32[56,768]{1,0:T(8,128)}, f32[56,768]{1,0:T(8,128)S(1)}, u32[]{:S(2)}, u32[]{:S(2)}) collective-permute-start(f32[56,768]{1,0:T(8,128)} %get-tuple-element.102), channel_id=1, source_target_pairs={{0,20},{4,16},{8,28},{12,24},{16,4},{20,0},{24,12},{28,8},{1,21},{... | collective-permute-start | bytes 516104 | tf_op jit(solution)/shard_map/ppermute | solution.py:419
  159.4 21.5 %collective-permute-start.33 = (f32[56,768]{1,0:T(8,128)}, f32[56,768]{1,0:T(8,128)S(1)}, u32[]{:S(2)}, u32[]{:S(2)}) collective-permute-start(f32[56,768]{1,0:T(8,128)} %get-tuple-element.103), channel_id=1, source_target_pairs={{0,24},{4,28},{8,16},{12,20},{16,8},{20,12},{24,0},{28,4},{1,25},{... | collective-permute-start | bytes 516104 | tf_op jit(solution)/shard_map/ppermute | solution.py:419
  161.8 19.0 %collective-permute-start.34 = (f32[56,768]{1,0:T(8,128)}, f32[56,768]{1,0:T(8,128)S(1)}, u32[]{:S(2)}, u32[]{:S(2)}) collective-permute-start(f32[56,768]{1,0:T(8,128)} %get-tuple-element.104), channel_id=1, source_target_pairs={{0,28},{4,24},{8,20},{12,16},{16,12},{20,8},{24,4},{28,0},{1,29},{... | collective-permute-start | bytes 516104 | tf_op jit(solution)/shard_map/ppermute | solution.py:419
  198.4 134.3 %reduce-scatter.4.cloned.1.call-start = ((), (), s32[]{:S(2)}) async-start(), calls=%async_computation.3 | async-start | bytes 3932160 | tf_op jit(solution)/shard_map/reduce_scatter | solution.py:458
  209.0 15.6 %collective-permute-start.15 = (f32[64,768]{1,0:T(8,128)}, f32[64,768]{1,0:T(8,128)S(1)}, u32[]{:S(2)}, u32[]{:S(2)}) collective-permute-start(f32[64,768]{1,0:T(8,128)} %get-tuple-element.79), channel_id=1, source_target_pairs={{0,8},{4,12},{8,0},{12,4},{16,24},{20,28},{24,16},{28,20},{1,9},{5... | collective-permute-start | bytes 589832 | tf_op jit(solution)/shard_map/ppermute | solution.py:419
  214.5 14.4 %collective-permute-start.16 = (f32[64,768]{1,0:T(8,128)}, f32[64,768]{1,0:T(8,128)S(1)}, u32[]{:S(2)}, u32[]{:S(2)}) collective-permute-start(f32[64,768]{1,0:T(8,128)} %get-tuple-element.80), channel_id=1, source_target_pairs={{0,12},{4,8},{8,4},{12,0},{16,28},{20,24},{24,20},{28,16},{1,13},{... | collective-permute-start | bytes 589832 | tf_op jit(solution)/shard_map/ppermute | solution.py:419
  214.5 25.0 %collective-permute-start.17 = (f32[64,768]{1,0:T(8,128)}, f32[64,768]{1,0:T(8,128)S(1)}, u32[]{:S(2)}, u32[]{:S(2)}) collective-permute-start(f32[64,768]{1,0:T(8,128)} %get-tuple-element.81), channel_id=1, source_target_pairs={{0,16},{4,20},{8,24},{12,28},{16,0},{20,4},{24,8},{28,12},{1,17},{... | collective-permute-start | bytes 589832 | tf_op jit(solution)/shard_map/ppermute | solution.py:419
  217.0 27.0 %collective-permute-start.18 = (f32[64,768]{1,0:T(8,128)}, f32[64,768]{1,0:T(8,128)S(1)}, u32[]{:S(2)}, u32[]{:S(2)}) collective-permute-start(f32[64,768]{1,0:T(8,128)} %get-tuple-element.82), channel_id=1, source_target_pairs={{0,20},{4,16},{8,28},{12,24},{16,4},{20,0},{24,12},{28,8},{1,21},{... | collective-permute-start | bytes 589832 | tf_op jit(solution)/shard_map/ppermute | solution.py:419
  218.3 25.7 %collective-permute-start.19 = (f32[64,768]{1,0:T(8,128)}, f32[64,768]{1,0:T(8,128)S(1)}, u32[]{:S(2)}, u32[]{:S(2)}) collective-permute-start(f32[64,768]{1,0:T(8,128)} %get-tuple-element.83), channel_id=1, source_target_pairs={{0,24},{4,28},{8,16},{12,20},{16,8},{20,12},{24,0},{28,4},{1,25},{... | collective-permute-start | bytes 589832 | tf_op jit(solution)/shard_map/ppermute | solution.py:419
  224.6 19.4 %collective-permute-start.20 = (f32[64,768]{1,0:T(8,128)}, f32[64,768]{1,0:T(8,128)S(1)}, u32[]{:S(2)}, u32[]{:S(2)}) collective-permute-start(f32[64,768]{1,0:T(8,128)} %get-tuple-element.84), channel_id=1, source_target_pairs={{0,28},{4,24},{8,20},{12,16},{16,12},{20,8},{24,4},{28,0},{1,29},{... | collective-permute-start | bytes 589832 | tf_op jit(solution)/shard_map/ppermute | solution.py:419
  263.1 106.4 %reduce-scatter.6.cloned.1.call-start = ((), (), s32[]{:S(2)}) async-start(), calls=%async_computation.4 | async-start | bytes 3932160 | tf_op jit(solution)/shard_map/reduce_scatter | solution.py:458
  273.6 15.3 %collective-permute-start.22 = (f32[64,768]{1,0:T(8,128)}, f32[64,768]{1,0:T(8,128)S(1)}, u32[]{:S(2)}, u32[]{:S(2)}) collective-permute-start(f32[64,768]{1,0:T(8,128)} %get-tuple-element.89), channel_id=1, source_target_pairs={{0,8},{4,12},{8,0},{12,4},{16,24},{20,28},{24,16},{28,20},{1,9},{5... | collective-permute-start | bytes 589832 | tf_op jit(solution)/shard_map/ppermute | solution.py:419
  279.2 14.8 %collective-permute-start.23 = (f32[64,768]{1,0:T(8,128)}, f32[64,768]{1,0:T(8,128)S(1)}, u32[]{:S(2)}, u32[]{:S(2)}) collective-permute-start(f32[64,768]{1,0:T(8,128)} %get-tuple-element.90), channel_id=1, source_target_pairs={{0,12},{4,8},{8,4},{12,0},{16,28},{20,24},{24,20},{28,16},{1,13},{... | collective-permute-start | bytes 589832 | tf_op jit(solution)/shard_map/ppermute | solution.py:419
  280.1 24.7 %collective-permute-start.24 = (f32[64,768]{1,0:T(8,128)}, f32[64,768]{1,0:T(8,128)S(1)}, u32[]{:S(2)}, u32[]{:S(2)}) collective-permute-start(f32[64,768]{1,0:T(8,128)} %get-tuple-element.91), channel_id=1, source_target_pairs={{0,16},{4,20},{8,24},{12,28},{16,0},{20,4},{24,8},{28,12},{1,17},{... | collective-permute-start | bytes 589832 | tf_op jit(solution)/shard_map/ppermute | solution.py:419
  282.1 26.9 %collective-permute-start.25 = (f32[64,768]{1,0:T(8,128)}, f32[64,768]{1,0:T(8,128)S(1)}, u32[]{:S(2)}, u32[]{:S(2)}) collective-permute-start(f32[64,768]{1,0:T(8,128)} %get-tuple-element.92), channel_id=1, source_target_pairs={{0,20},{4,16},{8,28},{12,24},{16,4},{20,0},{24,12},{28,8},{1,21},{... | collective-permute-start | bytes 589832 | tf_op jit(solution)/shard_map/ppermute | solution.py:419
  283.3 25.7 %collective-permute-start.26 = (f32[64,768]{1,0:T(8,128)}, f32[64,768]{1,0:T(8,128)S(1)}, u32[]{:S(2)}, u32[]{:S(2)}) collective-permute-start(f32[64,768]{1,0:T(8,128)} %get-tuple-element.93), channel_id=1, source_target_pairs={{0,24},{4,28},{8,16},{12,20},{16,8},{20,12},{24,0},{28,4},{1,25},{... | collective-permute-start | bytes 589832 | tf_op jit(solution)/shard_map/ppermute | solution.py:419
  289.0 20.1 %collective-permute-start.27 = (f32[64,768]{1,0:T(8,128)}, f32[64,768]{1,0:T(8,128)S(1)}, u32[]{:S(2)}, u32[]{:S(2)}) collective-permute-start(f32[64,768]{1,0:T(8,128)} %get-tuple-element.94), channel_id=1, source_target_pairs={{0,28},{4,24},{8,20},{12,16},{16,12},{20,8},{24,4},{28,0},{1,29},{... | collective-permute-start | bytes 589832 | tf_op jit(solution)/shard_map/ppermute | solution.py:419
  (46 other events, 1081.0 us)
Sparse Core Ops, SparseCore 0:
  198.5 38.1 reduce-scatter.7
  263.2 41.9 reduce-scatter.3
  328.3 41.1 reduce-scatter.5

commit v2 on v1

v2 whole, which is shorter than its diff:
```python
import functools
import math

import jax
import jax.numpy as jnp
import numpy as np
from jax import lax
from jax.experimental import pallas as pl
from jax.experimental.pallas import tpu as pltpu
from jax.sharding import PartitionSpec as P

NLON = 1440
NLAT = 720
MAXM = 720
LEV = 2
DAYS = 8
S = 16
LANES = 128
HALF = 64
VMEM_LIMIT = 56 * 1024 * 1024
PARTS = (10, 8, 5)


def up(value, step):
    return -(-value // step) * step


class Group:
    def __init__(self, start, rows):
        self.start, self.rows = start, rows
        self.row_pad = up(rows, 8)
        self.stride = up(rows, 16)


class Plan:
    def __init__(self, rows, lons, owned, lon_count, lat_count):
        self.rows, self.lons, self.owned = rows, lons, owned
        self.n, self.lat_count = lon_count, lat_count
        self.cols = 2 * S // lon_count
        self.full, self.rem = divmod(lons, LANES)
        assert 0 < self.rem < HALF
        self.tails = -(-self.cols // 2)
        self.blocks = self.cols * self.full + self.tails
        self.depth = lon_count * (self.full * LANES + HALF)
        self.tile = 64 if rows > 64 else up(rows, 16)
        cut = up(rows // 4, self.tile)
        spans = [(0, cut), (cut, rows)] if cut < rows else [(0, rows)]
        self.groups = [Group(a, b - a) for a, b in spans]
        self.share = owned * MAXM // lat_count
        self.first = [self.share * t // MAXM for t in range(lat_count)]
        last = [-(-self.share * (t + 1) // MAXM) for t in range(lat_count)]
        self.cover = max(b - a for a, b in zip(self.first, last))
        weights = PARTS
        cuts = [round(self.cover * sum(weights[:i]) / sum(weights)) for i in range(len(weights) + 1)]
        self.sizes = [b - a for a, b in zip(cuts, cuts[1:]) if b > a]
        self.starts = [sum(self.sizes[:i]) for i in range(len(self.sizes))]
        self.position_count = [lat_count * s for s in self.sizes]
        self.position_start = [lat_count * s for s in self.starts]
        slots = []
        for start, size in zip(self.starts, self.sizes):
            for t in range(lat_count):
                slots += [self.first[t] + start + i for i in range(size)]
        self.slots = slots
        self.positions = len(slots)
        self.height = self.groups[0].row_pad
        assert self.positions <= 2 * self.height
        self.held_rows = 2 * self.height
        pick = np.zeros((self.held_rows, owned), np.float32)
        absent = np.full((self.held_rows, 1), -1.0, np.float32)
        for p, slot in enumerate(slots):
            if slot < owned:
                pick[p, slot], absent[p] = 1.0, 0.0
        self.pick, self.absent = pick, absent


def lane_iota(shape):
    return lax.broadcasted_iota(jnp.int32, shape, len(shape) - 1)


def cost(us):
    return pl.CostEstimate(flops=0, bytes_accessed=int(us * 3.6e6), transcendentals=0)


def sincos(x):
    r = x - NLON * jnp.floor(x * (1.0 / NLON) + 0.5)
    q = jnp.floor(r * (4.0 / NLON) + 0.5)
    t = (r - q * (NLON // 4)) * (2.0 * math.pi / NLON)
    t2 = t * t
    s = t * (1.0 + t2 * (-1.0 / 6 + t2 * (1.0 / 120 + t2 * (-1.0 / 5040 + t2 * (1.0 / 362880)))))
    c = 1.0 + t2 * (
        -0.5 + t2 * (1.0 / 24 + t2 * (-1.0 / 720 + t2 * (1.0 / 40320 + t2 * (-1.0 / 3628800))))
    )
    size = jnp.abs(q)
    odd, flip = size == 1.0, size == 2.0
    cosine = jnp.where(odd, -q * s, jnp.where(flip, -c, c))
    sine = jnp.where(odd, q * c, jnp.where(flip, -s, s))
    return cosine, sine


def flux_kernel(plan, group, lev_ref, slot_ref, pick_ref, absent_ref, u_ref, v_ref, z_ref, *refs):
    out, scratch = refs
    tile = plan.tile
    row = lax.broadcasted_iota(jnp.int32, (S, 1), 0)
    level = jnp.zeros((S, 1), jnp.int32)
    for s in range(S):
        level = jnp.where(row == s, lev_ref[s], level)

    def eddy(x):
        out = x
        for a in range(LEV):
            mask = (level == a).astype(jnp.float32)[None]
            mean = jnp.sum(x * mask, axis=1, keepdims=True) * (1.0 / DAYS)
            out = out - mean * mask
        return out

    eddy_z = eddy(z_ref[...])
    for f, ref in enumerate((u_ref, v_ref)):
        flux = eddy(ref[...]) * eddy_z
        for b in range(plan.full):
            part = flux[:, :, b * LANES : (b + 1) * LANES]
            scratch[f, b] = part.reshape(tile * S, LANES)
        part = flux[:, :, plan.full * LANES :]
        scratch[f, plan.full, :, 0 : plan.rem] = part.reshape(tile * S, plan.rem)
    first = lax.axis_index("lat") * plan.rows + group.start + pl.program_id(0) * tile
    index = first + lax.broadcasted_iota(jnp.int32, (tile, 1), 0)
    _, cosine = sincos((index.astype(jnp.float32) + 0.5) * (NLON / (2.0 * NLAT)))
    lane = lane_iota((tile, LANES))
    per_field = plan.n // 2
    if group.start == 0:
        wave = slot_ref[...].astype(jnp.float32)
        column = jnp.sum(pick_ref[...] * wave, axis=1, keepdims=True) + absent_ref[...]
    for k in range(plan.n):
        field, sample = k // per_field, k % per_field * plan.cols
        packed = [jnp.zeros((tile, LANES), jnp.float32) for _ in range(plan.tails)]
        for c in range(plan.cols):
            rows = pl.ds(sample + c, tile, stride=S)
            for b in range(plan.full):
                out[k, c * plan.full + b] = scratch[field, b, rows, :] * cosine
            tail = jnp.where(lane < plan.rem, scratch[field, plan.full, rows, :] * cosine, 0.0)
            if c % 2:
                tail = pltpu.roll(tail, HALF, 1)
            packed[c // 2] = packed[c // 2] + tail
        if group.start == 0:
            for i in range(2):
                spare = (lane == (i + 1) * HALF - 1)[: plan.height]
                held = column[i * plan.height : (i + 1) * plan.height]
                packed[0] = jnp.where(spare, held, packed[0][: plan.height])
        for i, value in enumerate(packed):
            out[k, plan.cols * plan.full + i] = value


def flux_call(plan, group, level, slots, u, v, z):
    tile = plan.tile
    skip = group.start // tile
    if skip == 0:
        assert group.row_pad == tile
    field = pl.BlockSpec((tile, S, plan.lons), lambda i: (i + skip, 0, 0))
    fixed = lambda x: pl.BlockSpec(x.shape, lambda i: (0, 0))
    pick, absent = jnp.asarray(plan.pick), jnp.asarray(plan.absent)
    return pl.pallas_call(
        functools.partial(flux_kernel, plan, group),
        grid=(pl.cdiv(group.row_pad, tile),),
        in_specs=[pl.BlockSpec(memory_space=pltpu.SMEM)]
        + [fixed(x) for x in (slots, pick, absent)]
        + [field] * 3,
        out_specs=pl.BlockSpec((plan.n, plan.blocks, tile, LANES), lambda i: (0, 0, i, 0)),
        out_shape=jax.ShapeDtypeStruct(
            (plan.n, plan.blocks, group.row_pad, LANES), jnp.float32
        ),
        scratch_shapes=[pltpu.VMEM((2, plan.full + 1, tile * S, LANES), jnp.float32)],
        compiler_params=pltpu.CompilerParams(vmem_limit_bytes=VMEM_LIMIT),
        cost_estimate=cost(4 * group.rows / 48),
        name="eddy_flux",
    )(level, slots, pick, absent, u, v, z)


def table_kernel(plan, got_ref, *refs):
    parts = len(plan.sizes)
    highs, lows, held = refs[:parts], refs[parts : 2 * parts], refs[-1]
    for k in range(plan.n):
        tail = got_ref[k, 0]
        held[k, 0 : plan.height] = tail
        held[k, plan.height :] = pltpu.roll(tail, HALF, 1)

    @pl.loop(0, plan.n)
    def _(k):
        for j, count in enumerate(plan.position_count):
            start = plan.position_start[j]
            wave = held[k, start : start + count, HALF - 1 : HALF]
            weight = jnp.where(wave >= 0.0, 1.0 / NLON, 0.0)
            wave = jnp.maximum(wave, 0.0)
            lane = lane_iota((count, LANES))
            source = lane.astype(jnp.float32) * plan.lons
            turn_cos, turn_sin = sincos(wave * source)
            base = []
            for b in range(plan.full):
                c, s = sincos(wave * (lane + b * LANES).astype(jnp.float32))
                base.append((c * weight, s * weight))
            tail_lane = lane_iota((count, HALF))
            c, s = sincos(wave * (tail_lane + plan.full * LANES).astype(jnp.float32))
            tail_weight = jnp.where(tail_lane < plan.rem, weight, 0.0)
            c, s = c * tail_weight, s * tail_weight

            def put(where, cosine, sine):
                for row, value in ((0, cosine), (count, sine)):
                    high = value.astype(jnp.bfloat16)
                    highs[j][k, row : row + count, where] = high
                    lows[j][k, row : row + count, where] = (
                        value - high.astype(jnp.float32)
                    ).astype(jnp.bfloat16)

            for src in range(plan.n):
                tc, ts = turn_cos[:, src : src + 1], turn_sin[:, src : src + 1]
                for b in range(plan.full):
                    at = (src * plan.full + b) * LANES
                    bc, bs = base[b]
                    put(slice(at, at + LANES), tc * bc - ts * bs, ts * bc + tc * bs)
            for src in range(0, plan.n, 2):
                at = plan.n * plan.full * LANES + src * HALF
                both = []
                for x in (src, src + 1):
                    tc, ts = turn_cos[:, x : x + 1], turn_sin[:, x : x + 1]
                    both.append((tc * c - ts * s, ts * c + tc * s))
                put(
                    slice(at, at + LANES),
                    jnp.concatenate([both[0][0], both[1][0]], axis=1),
                    jnp.concatenate([both[0][1], both[1][1]], axis=1),
                )


def table_call(plan, got):
    at = plan.cols * plan.full
    tail = pl.BlockSpec((plan.n, 1, plan.height, LANES), lambda i: (0, at, 0, 0))
    shapes = [
        jax.ShapeDtypeStruct((plan.n, 2 * count, plan.depth), jnp.bfloat16)
        for count in plan.position_count
    ]
    out = pl.pallas_call(
        functools.partial(table_kernel, plan),
        grid=(1,),
        in_specs=[tail],
        out_specs=[pl.BlockSpec(x.shape, lambda i: (0, 0, 0)) for x in shapes * 2],
        out_shape=shapes * 2,
        scratch_shapes=[pltpu.VMEM((plan.n, plan.held_rows, LANES), jnp.float32)],
        compiler_params=pltpu.CompilerParams(vmem_limit_bytes=VMEM_LIMIT),
        cost_estimate=cost(12),
        name="wave_table",
    )(got)
    parts = len(plan.sizes)
    return list(zip(out[:parts], out[parts:]))


def split_kernel(plan, group, got_ref, high, low):
    def put(rows, lanes, value):
        top = value.astype(jnp.bfloat16)
        high[rows, lanes] = top
        low[rows, lanes] = (value - top.astype(jnp.float32)).astype(jnp.bfloat16)

    base = plan.n * plan.full * LANES
    for c in range(plan.cols):
        rows = slice(c * group.stride, c * group.stride + group.row_pad)
        for k in range(plan.n):
            for b in range(plan.full):
                at = (k * plan.full + b) * LANES
                put(rows, slice(at, at + LANES), got_ref[k, c * plan.full + b])
        for k in range(0, plan.n, 2):
            at = base + k * HALF
            tail = plan.cols * plan.full + c // 2
            first, second = got_ref[k, tail], got_ref[k + 1, tail]
            lane = lane_iota(first.shape)
            if c % 2:
                first = pltpu.roll(first, HALF, 1)
            else:
                second = pltpu.roll(second, HALF, 1)
            put(rows, slice(at, at + LANES), jnp.where(lane < HALF, first, second))


def split_call(plan, group, got):
    shape = jax.ShapeDtypeStruct((plan.cols * group.stride, plan.depth), jnp.bfloat16)
    return pl.pallas_call(
        functools.partial(split_kernel, plan, group),
        out_shape=[shape, shape],
        compiler_params=pltpu.CompilerParams(vmem_limit_bytes=VMEM_LIMIT),
        cost_estimate=cost(7.0 * group.rows / plan.rows),
        name="split_circles",
    )(got)


def dft_kernel(plan, th_ref, tl_ref, *refs):
    circles, out = refs[:-1], refs[-1]
    count = th_ref.shape[1]
    shape = (plan.n * count, plan.depth)
    th, tl = th_ref[...].reshape(shape), tl_ref[...].reshape(shape)
    dot = functools.partial(
        lax.dot_general,
        dimension_numbers=(((1,), (1,)), ((), ())),
        preferred_element_type=jnp.float32,
    )
    at = 0
    for fh_ref, fl_ref in zip(circles[::2], circles[1::2]):
        fh, fl = fh_ref[...], fl_ref[...]
        total = dot(th, fh) + (dot(th, fl) + dot(tl, fh))
        for k in range(plan.n):
            out[k, :, at : at + fh.shape[0]] = total[k * count : (k + 1) * count]
        at += fh.shape[0]


def dft_call(plan, table, circles):
    count = table[0].shape[1]
    lanes = sum(pair[0].shape[0] for pair in circles)
    return pl.pallas_call(
        functools.partial(dft_kernel, plan),
        out_shape=jax.ShapeDtypeStruct((plan.n, count, lanes), jnp.float32),
        compiler_params=pltpu.CompilerParams(vmem_limit_bytes=VMEM_LIMIT),
        cost_estimate=cost(count * lanes * 27.0 / (184 * 768)),
        name="dft",
    )(*table, *[x for pair in circles for x in pair])


def legendre_kernel(plan, part, wide, buffers, sets, wave_ref, scale_ref, *refs):
    pieces, refs = refs[:sets], refs[sets:]
    tables, edges = refs[:2], refs[2:4]
    send_ref, keep_ref, right, held, sems = refs[4:]
    size, start = plan.sizes[part], plan.starts[part]
    count, offset = plan.position_count[part], plan.position_start[part]
    total = plan.owned * MAXM
    band = lax.axis_index("lat")
    inner = wide - LANES
    step = 2 * LANES
    begins = range(0, wide, step)
    half = count // 2

    def place(p):
        kept = p // half
        q = lax.rem(p, half)
        t = lax.bitwise_xor(q // size * 2 + 1 - kept, band)
        i = lax.rem(q, size)
        slot = (plan.share * t) // MAXM + start + i
        column = jnp.minimum(slot, plan.owned - 1) * MAXM
        shift = lax.rem(column, LANES)
        position = t * size + i
        wave = wave_ref[offset + position]
        lowest = jnp.where(wave < 0, wide, wave + shift) // step
        return position, column - shift, shift, wave, lowest

    def copies(p, act):
        _, base, _, _, lowest = place(p)
        buffer = lax.rem(p, buffers)
        whole = base + wide <= total

        def copy(f, slot, source, at, width):
            into = held.at[buffer, f, :, pl.ds(at, width)]
            act(pltpu.make_async_copy(source, into, sems.at[buffer, f, slot]))

        for i, at in enumerate(begins):

            @pl.when((lowest == i) & whole)
            def _():
                column = pl.multiple_of(base + at, LANES)
                for f in range(2):
                    copy(f, 0, tables[f].at[:, pl.ds(column, wide - at)], at, wide - at)

            @pl.when((lowest == i) & jnp.logical_not(whole))
            def _():
                column = pl.multiple_of(base + at, LANES)
                for f in range(2):
                    if at < inner:
                        copy(f, 0, tables[f].at[:, pl.ds(column, inner - at)], at, inner - at)
                    copy(f, 1, edges[f], inner, LANES)

    for p in range(min(buffers - 1, count)):
        copies(jnp.int32(p), lambda c: c.start())

    per_field = plan.n // 2
    scale = scale_ref[...]
    for k in range(plan.n):
        field, sample = k // per_field, k % per_field * plan.cols
        for cs in range(2):
            factor = (-1.0 if cs == 0 else 1.0) if field else scale
            imaginary = field if cs else 1 - field
            for c in range(plan.cols):
                values = []
                base = 0
                for i, group in enumerate(plan.groups):
                    at = base + c * group.stride
                    block = pieces[i if sets > 1 else 0]
                    values.append(block[k, cs * count : (cs + 1) * count, at : at + group.rows])
                    base += plan.cols * group.stride if sets == 1 else 0
                value = values[0] if len(values) == 1 else jnp.concatenate(values, axis=1)
                value = value * factor
                rows = pl.ds(imaginary * S + sample + c, count, stride=2 * S)
                for b, a in enumerate(range(0, plan.rows, LANES)):
                    width = min(LANES, plan.rows - a)
                    right[field, b, rows, 0:width] = value[:, a : a + width]

    blocks = pl.cdiv(plan.rows, LANES)
    lane = lane_iota((2 * S, LANES))

    def run(first, out_ref):
        @pl.loop(0, half)
        def _(q):
            p = first + q

            @pl.when(p + buffers - 1 < count)
            def _():
                copies(p + buffers - 1, lambda c: c.start())

            copies(p, lambda c: c.wait())
            buffer = lax.rem(p, buffers)
            position, _, shift, wave, lowest = place(p)
            rows = pl.ds(pl.multiple_of(position * 2 * S, 2 * S), 2 * S)

            for i, at in enumerate(begins):

                @pl.when(lowest == i)
                def _():
                    sums = None
                    for f in range(2):
                        row = [right[f, b, rows, :] for b in range(blocks)]
                        left = jnp.concatenate(row, axis=1)[:, : plan.rows].astype(jnp.bfloat16)
                        term = jnp.dot(
                            left, held[buffer, f, :, at:], preferred_element_type=jnp.float32
                        )
                        sums = term if sums is None else sums + term
                    turned = [
                        pltpu.roll(sums[:, v : v + LANES], lax.rem(LANES - shift, LANES), 1)
                        for v in range(0, wide - at, LANES)
                    ]
                    for v in range(inner // LANES):
                        here = slice(v * LANES, (v + 1) * LANES)
                        if (v + 1) * LANES < at:
                            out_ref[q, :, here] = jnp.zeros((2 * S, LANES), jnp.float32)
                            continue
                        w = v - at // LANES
                        below = turned[max(w, 0)]
                        moved = jnp.where(lane < LANES - shift, below, turned[w + 1])
                        degree = lane + v * LANES
                        keep = (degree >= wave) & (degree < MAXM)
                        out_ref[q, :, here] = jnp.where(keep, moved, 0.0)

            @pl.when(wave < 0)
            def _():
                out_ref[q] = jnp.zeros((2 * S, inner), jnp.float32)

    run(0, send_ref)
    run(half, keep_ref)


def legendre_call(plan, part, wave, scale, pieces, tables, edges):
    wide = up(MAXM, LANES) + LANES
    buffers = 8
    count = plan.position_count[part]
    vmem = pl.BlockSpec(memory_space=pltpu.VMEM)
    hbm = pl.BlockSpec(memory_space=pl.ANY)
    blocks = pl.cdiv(plan.rows, LANES)
    shape = jax.ShapeDtypeStruct((count // 2, 2 * S, wide - LANES), jnp.float32)
    return pl.pallas_call(
        functools.partial(legendre_kernel, plan, part, wide, buffers, len(pieces)),
        in_specs=[pl.BlockSpec(memory_space=pltpu.SMEM), vmem]
        + [vmem] * len(pieces)
        + [hbm, hbm]
        + [hbm, hbm],
        out_specs=[vmem, vmem],
        out_shape=[shape, shape],
        scratch_shapes=[
            pltpu.VMEM((2, blocks, count * 2 * S, LANES), jnp.float32),
            pltpu.VMEM((buffers, 2, plan.rows, wide), jnp.bfloat16),
            pltpu.SemaphoreType.DMA((buffers, 2, 2)),
        ],
        compiler_params=pltpu.CompilerParams(vmem_limit_bytes=VMEM_LIMIT),
        cost_estimate=cost(0.6 * count),
        name="legendre",
    )(wave, scale, *pieces, *tables, *edges)


def reduce_scatter(plan, size, send, keep):
    bit = 1
    while True:
        got = lax.ppermute(send, "lat", [(t, t ^ bit) for t in range(plan.lat_count)])
        total = keep + got
        bit *= 2
        if bit == plan.lat_count:
            return total
        total = total.reshape(-1, 2, size, *total.shape[1:])
        send = total[:, 1].reshape(-1, *total.shape[3:])
        keep = total[:, 0].reshape(-1, *total.shape[3:])


def after(x, *others):
    return lax.optimization_barrier((x, *others))[0]


def exchange(x):
    return lax.all_to_all(x, "lon", 0, 0, tiled=True)


def body(wind_u, wind_v, vorticity, sample_level, slot_wavenumber, legendre_p, legendre_h):
    rows, lons = wind_u.shape[0], wind_u.shape[1]
    lon_count, lat_count = lax.axis_size("lon"), lax.axis_size("lat")
    plan = Plan(rows, lons, slot_wavenumber.shape[0], lon_count, lat_count)
    wave = jnp.concatenate([slot_wavenumber, jnp.full((1,), -1, jnp.int32)])
    wave = wave[jnp.array([min(x, plan.owned) for x in plan.slots], jnp.int32)]
    fields = [jnp.transpose(x, (0, 2, 1)) for x in (wind_u, wind_v, vorticity)]
    got = []
    for group in plan.groups:
        sent = flux_call(plan, group, sample_level, slot_wavenumber[None, :], *fields)
        got.append(exchange(after(sent, *got[-1:])))
    tables = table_call(plan, got[0])
    circles = [split_call(plan, group, pieces) for group, pieces in zip(plan.groups, got)]
    scale = (jnp.maximum(wave, 0).astype(jnp.float32) / MAXM)[:, None]
    edge_start = plan.owned * MAXM // LANES * LANES
    edges = []
    for table in (legendre_p, legendre_h):
        edge = table[:, edge_start:]
        edges.append(jnp.pad(edge, ((0, 0), (0, LANES - edge.shape[1]))))
    onehot = (sample_level[:, None] == jnp.arange(LEV, dtype=jnp.int32)[None, :]).astype(
        jnp.float32
    )
    coeffs = []
    for pair in circles:
        sent = dft_call(plan, tables[0], [pair])
        coeffs.append(exchange(after(sent, *(coeffs or got)[-1:])))
    later = [dft_call(plan, table, circles) for table in tables[1:]]
    powers = []
    for part, size in enumerate(plan.sizes):
        first, count = plan.position_start[part], plan.position_count[part]
        following = later[part : part + 1]
        if following:
            following = [exchange(after(following[0], coeffs[-1]))]
        factor = scale[first : first + count]
        send, keep = legendre_call(
            plan, part, wave, factor, coeffs, (legendre_p, legendre_h), edges
        )
        coeffs = following
        mine = reduce_scatter(plan, size, send, keep)
        power = mine[:, :S] ** 2 + mine[:, S:] ** 2
        powers.append(
            jnp.einsum("isx,sl->lix", power, onehot, precision=lax.Precision.HIGHEST) / DAYS
        )
    spectra = jnp.concatenate(powers, axis=1)[:, :, :MAXM].reshape(LEV, plan.cover * MAXM)
    begin = jnp.array([plan.share * t - f * MAXM for t, f in enumerate(plan.first)], jnp.int32)
    return lax.dynamic_slice_in_dim(spectra, begin[lax.axis_index("lat")], plan.share, 1)


def solution(mesh):
    placed = (
        P("lat", "lon", None),
        P("lat", "lon", None),
        P("lat", "lon", None),
        P(),
        P("lon"),
        P("lat", "lon"),
        P("lat", "lon"),
    )
    return jax.shard_map(
        body, mesh=mesh, in_specs=placed, out_specs=P(None, ("lon", "lat")), check_vma=False
    )
```

time: 380 us -> 302 us (0.79)
  waiting for transfers between devices: 166 us -> 129 us
  starting transfers between devices: 65.7 us -> 30.5 us
  between operations: 15.5 us -> 2.21 us
  Pallas kernels: 112 us -> 118 us
  other arithmetic: 2.43 us -> 7.93 us
    ppermute x35 -> x6, waiting for transfers between devices: 131 us -> 23.2 us  [reduce_scatter(): lax.ppermute(send, 'lat', [(t, t ^ bit) for t in range(plan.lat_count)])]
    all_to_all x0 -> x6, waiting for transfers between devices: none -> 106 us  [exchange(): return lax.all_to_all(x, 'lon', 0, 0, tiled=True)]
    ppermute x35 -> x6, starting transfers between devices: 65.4 us -> 4.01 us  [reduce_scatter(): lax.ppermute(send, 'lat', [(t, t ^ bit) for t in range(plan.lat_count)])]
    reduce_scatter x3 -> x0, waiting for transfers between devices: 35.3 us -> none  [body(): mine = lax.psum_scatter(sums, 'lat', scatter_dimension=0, tiled=True)]
    all_to_all x0 -> x6, starting transfers between devices: none -> 26.5 us  [exchange(): return lax.all_to_all(x, 'lon', 0, 0, tiled=True)]
    add x0 -> x6, other arithmetic: none -> 7.78 us  [reduce_scatter(): total = keep + got]
    pallas_call x3, Pallas kernels: 53.2 us -> 57.6 us  [legendre_call(): pl.pallas_call(functools.partial(legendre_kernel, plan, part, wide, buffe...]
    pallas_call x6 -> x8, Pallas kernels: 47.4 us -> 49.1 us  [the longest x4 27.3 us: dft_call(): pl.pallas_call(functools.partial(dft_kernel, plan), out_shape=jax.ShapeDt...]
  transfers between devices with their start and end apart: 38 -> 12, of which waited for: 17 -> 8; matrix products, arithmetic and copies ran while one was open for 2% -> 5% of each run, Pallas kernels for 19% -> 37%
where the time goes in v2:
time: 302 us; the launch traced here: 301 us
  waiting for transfers between devices  129 us (43%)
  Pallas kernels  118 us (39%)
  starting transfers between devices  30.5 us (10%)
  local copies, waits for them, and re-layouts  11.7 us (4%)
  other arithmetic  7.93 us (3%)
    all_to_all x6, waiting for transfers between devices, exchange(): return lax.all_to_all(x, 'lon', 0, 0, tiled=True)  106 us
    pallas_call x3, Pallas kernels, legendre_call(): pl.pallas_call(functools.partial(legendre_kernel, plan, part, wide, buffe...  57.6 us
    pallas_call x4, Pallas kernels, dft_call(): pl.pallas_call(functools.partial(dft_kernel, plan), out_shape=jax.ShapeDt...  27.3 us
    all_to_all x6, starting transfers between devices, exchange(): return lax.all_to_all(x, 'lon', 0, 0, tiled=True)  26.5 us
    ppermute x6, waiting for transfers between devices, reduce_scatter(): lax.ppermute(send, 'lat', [(t, t ^ bit) for t in range(plan.lat_count)])  23.2 us
    pallas_call x2, Pallas kernels, flux_call(): pl.pallas_call(functools.partial(flux_kernel, plan, group), grid=(pl.cdiv...  15.1 us
    pallas_call x1, Pallas kernels, table_call(): pl.pallas_call(functools.partial(table_kernel, plan), grid=(1,), in_specs...  11.8 us
    add x6, other arithmetic, reduce_scatter(): total = keep + got  7.78 us
  transfers between devices with their start and end apart: 12, of which 8 were waited for; matrix products, arithmetic and copies ran while one was open for 5% of the time, Pallas kernels for 37%

profile of v2, /device:TPU:0, one launch (start us, length us, event | category | flops | bytes accessed | tf_op | source)
XLA Modules:
  0.0 300.9 jit_solution(13285136277355248864)
XLA Ops:
  0.0 6.1 %eddy_flux.2 = f32[8,6,64,128]{3,2,1,0:T(8,128)} custom-call(s32[16]{0:T(128)} %lev_ref.3, s32[1,90]{1,0:T(1,128)} %bitcast.51, f32[128,90]{1,0:T(8,128)} %constant.36.clone.pick_ref, f32[128,1]{1,0:T(8,128)} %constant.37.clone.absent_ref, f32[180,16,180]{2,1,0:T(8,128)} %bitcast.39, f32[180,16,180]{2,1,0:T(8,128)} %bitcast.41, f32[180,16,180]{2,1,0:T(8,128)} %bitcast.43), custom_call_target="tpu_custom_call" | custom-call | bytes 19200000 | tf_op jit(solution)/shard_map/eddy_flux/pallas_call | solution.py:160
  6.1 7.3 %all-to-all-start = ((f32[8,6,64,128]{3,2,1,0:T(8,128)}), f32[8,6,64,128]{3,2,1,0:T(8,128)S(1)}, u32[]{:S(2)}, u32[]{:S(2)}) async-start(f32[8,6,64,128]{3,2,1,0:T(8,128)} %eddy_flux.2), calls=%async_computation | async-start | bytes 3145728 | tf_op jit(solution)/shard_map/all_to_all | solution.py:494
  13.3 9.0 %eddy_flux.3 = f32[8,6,120,128]{3,2,1,0:T(8,128)} custom-call(s32[16]{0:T(128)} %lev_ref.3, s32[1,90]{1,0:T(1,128)} %bitcast.52, f32[128,90]{1,0:T(8,128)} %constant.36.clone.pick_ref, f32[128,1]{1,0:T(8,128)} %constant.37.clone.absent_ref, f32[180,16,180]{2,1,0:T(8,128)} %bitcast.40, f32[180,16,180]{2,1,0:T(8,128)} %bitcast.42, f32[180,16,180]{2,1,0:T(8,128)} %bitcast.44), custom_call_target="tpu_custom_call" | custom-call | bytes 34800000 | tf_op jit(solution)/shard_map/eddy_flux/pallas_call | solution.py:160
  22.4 28.0 %all-to-all-done.got_ref = f32[8,6,64,128]{3,2,1,0:T(8,128)S(1)} async-done(((f32[8,6,64,128]{3,2,1,0:T(8,128)}), f32[8,6,64,128]{3,2,1,0:T(8,128)S(1)}, u32[]{:S(2)}, u32[]{:S(2)}) %all-to-all-start) | async-done | bytes 1572896 | tf_op jit(solution)/shard_map/all_to_all | solution.py:494
  51.5 4.4 %all-to-all-start.1 = ((f32[8,6,120,128]{3,2,1,0:T(8,128)}), f32[8,6,120,128]{3,2,1,0:T(8,128)}, u32[]{:S(2)}, u32[]{:S(2)}) async-start(f32[8,6,120,128]{3,2,1,0:T(8,128)} %eddy_flux.3), calls=%async_computation.1 | async-start | bytes 5898240 | tf_op jit(solution)/shard_map/all_to_all | solution.py:494
  56.0 11.8 %wave_table.1 = (bf16[8,80,1536]{2,1,0:T(8,128)(2,1)}, bf16[8,64,1536]{2,1,0:T(8,128)(2,1)}, bf16[8,40,1536]{2,1,0:T(8,128)(2,1)}, bf16[8,80,1536]{2,1,0:T(8,128...) custom-call(f32[8,6,64,128]{3,2,1,0:T(8,128)} %copy-done), custom_call_target="tpu_custom_call" | custom-call | bytes 43200000 | tf_op jit(solution)/shard_map/wave_table/pallas_call | solution.py:238
  67.7 2.8 split_circles.2
  70.5 5.1 %dft.4 = f32[8,80,256]{2,1,0:T(8,128)} custom-call(bf16[8,80,1536]{2,1,0:T(8,128)(2,1)} %get-tuple-element.26.th_ref, bf16[8,80,1536]{2,1,0:T(8,128)(2,1)} %get-tuple-element.27.tl_ref, bf16[256,1536]{1,0:T(8,128)(2,1)} %get-tuple-element.28.refs_0_, bf16[256,1536]{1,0:T(8,128)(2,1)} %get-tuple-element.29.refs_1_), custom_call_target="tpu_custom_call" | custom-call | bytes 14086956 | tf_op jit(solution)/shard_map/dft/pallas_call | solution.py:311
  75.7 46.3 %all-to-all-done.1.got_ref = f32[8,6,120,128]{3,2,1,0:T(8,128)} async-done(((f32[8,6,120,128]{3,2,1,0:T(8,128)}), f32[8,6,120,128]{3,2,1,0:T(8,128)}, u32[]{:S(2)}, u32[]{:S(2)}) %all-to-all-start.1) | async-done | bytes 2949152 | tf_op jit(solution)/shard_map/all_to_all | solution.py:494
  122.0 3.6 %all-to-all-start.2 = ((f32[8,80,256]{2,1,0:T(8,128)}), f32[8,80,256]{2,1,0:T(8,128)S(1)}, u32[]{:S(2)}, u32[]{:S(2)}) async-start(f32[8,80,256]{2,1,0:T(8,128)} %dft.4), calls=%async_computation.2 | async-start | bytes 1310720 | tf_op jit(solution)/shard_map/all_to_all | solution.py:494
  125.6 3.9 %split_circles.3 = (bf16[512,1536]{1,0:T(8,128)(2,1)}, bf16[512,1536]{1,0:T(8,128)(2,1)}) custom-call(f32[8,6,120,128]{3,2,1,0:T(8,128)} %all-to-all-done.1.got_ref), custom_call_target="tpu_custom_call" | custom-call | bytes 16240000 | tf_op jit(solution)/shard_map/split_circles/pallas_call | solution.py:280
  129.5 7.4 %dft.5 = f32[8,80,512]{2,1,0:T(8,128)} custom-call(bf16[8,80,1536]{2,1,0:T(8,128)(2,1)} %get-tuple-element.26.th_ref, bf16[8,80,1536]{2,1,0:T(8,128)(2,1)} %get-tuple-element.27.tl_ref, bf16[512,1536]{1,0:T(8,128)(2,1)} %get-tuple-element.32.refs_0_.refs_2_, bf16[512,1536]{1,0:T(8,128)(2,1)} %get-tuple-element.33.refs_1_.refs_3_), custom_call_target="tpu_custom_call" | custom-call | bytes 28173912 | tf_op jit(solution)/shard_map/dft/pallas_call | solution.py:311
  136.9 6.2 %all-to-all-done.2.refs_0_ = f32[8,80,256]{2,1,0:T(8,128)S(1)} async-done(((f32[8,80,256]{2,1,0:T(8,128)}), f32[8,80,256]{2,1,0:T(8,128)S(1)}, u32[]{:S(2)}, u32[]{:S(2)}) %all-to-all-start.2) | async-done | bytes 655392 | tf_op jit(solution)/shard_map/all_to_all | solution.py:494
  143.1 3.8 %all-to-all-start.3 = ((f32[8,80,512]{2,1,0:T(8,128)}), f32[8,80,512]{2,1,0:T(8,128)S(1)}, u32[]{:S(2)}, u32[]{:S(2)}) async-start(f32[8,80,512]{2,1,0:T(8,128)} %dft.5), calls=%async_computation.3 | async-start | bytes 2621440 | tf_op jit(solution)/shard_map/all_to_all | solution.py:494
  146.8 8.3 %dft.6 = f32[8,64,768]{2,1,0:T(8,128)} custom-call(bf16[8,64,1536]{2,1,0:T(8,128)(2,1)} %get-tuple-element.37.th_ref, bf16[8,64,1536]{2,1,0:T(8,128)(2,1)} %get-tuple-element.38.tl_ref, bf16[256,1536]{1,0:T(8,128)(2,1)} %get-tuple-element.28.refs_0_, bf16[256,1536]{1,0:T(8,128)(2,1)} %get-tuple-element.29.refs_1_, ...), custom_call_target="tpu_custom_call" | custom-call | bytes 33808696 | tf_op jit(solution)/shard_map/dft/pallas_call | solution.py:311
  155.2 23.1 %all-to-all-done.3.refs_1_ = f32[8,80,512]{2,1,0:T(8,128)S(1)} async-done(((f32[8,80,512]{2,1,0:T(8,128)}), f32[8,80,512]{2,1,0:T(8,128)S(1)}, u32[]{:S(2)}, u32[]{:S(2)}) %all-to-all-start.3) | async-done | bytes 1310752 | tf_op jit(solution)/shard_map/all_to_all | solution.py:494
  179.4 3.6 %all-to-all-start.4 = ((f32[8,64,768]{2,1,0:T(8,128)}), f32[8,64,768]{2,1,0:T(8,128)S(1)}, u32[]{:S(2)}, u32[]{:S(2)}) async-start(f32[8,64,768]{2,1,0:T(8,128)} %dft.6), calls=%async_computation.4 | async-start | bytes 3145728 | tf_op jit(solution)/shard_map/all_to_all | solution.py:494
  186.3 24.8 %legendre.3 = (f32[20,32,768]{2,1,0:T(8,128)}, f32[20,32,768]{2,1,0:T(8,128)}) custom-call(s32[92]{0:T(128)} %copy-done.7, f32[40,1]{1,0:T(8,128)} %copy.15.scale_ref, f32[8,80,256]{2,1,0:T(8,128)} %copy-done.4, f32[8,80,512]{2,1,0:T(8,128)} %copy-done.2, bf16[180,64800]{1,0:T(8,128)(2,1)} %refs_1_.3, bf16[180,64800]{1,0:T(8,128)(2,1)} %refs_2_.5, ...), custom_call_target="tpu_custom_call" | custom-call | bytes 86400000 | tf_op jit(solution)/shard_map/legendre/pallas_call | solution.py:457
  211.2 6.5 %dft.7 = f32[8,40,768]{2,1,0:T(8,128)} custom-call(bf16[8,40,1536]{2,1,0:T(8,128)(2,1)} %get-tuple-element.42.th_ref, bf16[8,40,1536]{2,1,0:T(8,128)(2,1)} %get-tuple-element.43.tl_ref, bf16[256,1536]{1,0:T(8,128)(2,1)} %get-tuple-element.28.refs_0_, bf16[256,1536]{1,0:T(8,128)(2,1)} %get-tuple-element.29.refs_1_, ...), custom_call_target="tpu_custom_call" | custom-call | bytes 21130434 | tf_op jit(solution)/shard_map/dft/pallas_call | solution.py:311
  217.6 2.5 all-to-all-done.4.refs_0_
  220.2 3.8 %all-to-all-start.5 = ((f32[8,40,768]{2,1,0:T(8,128)}), f32[8,40,768]{2,1,0:T(8,128)S(1)}, u32[]{:S(2)}, u32[]{:S(2)}) async-start(f32[8,40,768]{2,1,0:T(8,128)} %dft.7), calls=%async_computation.5 | async-start | bytes 1966080 | tf_op jit(solution)/shard_map/all_to_all | solution.py:494
  224.7 20.1 %legendre.4 = (f32[16,32,768]{2,1,0:T(8,128)}, f32[16,32,768]{2,1,0:T(8,128)}) custom-call(s32[92]{0:T(128)} %copy-done.7, f32[32,1]{1,0:T(8,128)} %copy.16.scale_ref, f32[8,64,768]{2,1,0:T(8,128)} %copy-done.1, bf16[180,64800]{1,0:T(8,128)(2,1)} %refs_1_.3, bf16[180,64800]{1,0:T(8,128)(2,1)} %refs_2_.5, bf16[180,128]{1,0:T(8,128)(2,1)} %pad.7.refs_4_.refs_3_, ...), custom_call_target="tpu_custom_call" | custom-call | bytes 69120000 | tf_op jit(solution)/shard_map/legendre/pallas_call | solution.py:457
  244.9 1.8 add.45
  247.8 1.5 collective-permute-start.1
  251.0 12.7 %legendre.5 = (f32[10,32,768]{2,1,0:T(8,128)}, f32[10,32,768]{2,1,0:T(8,128)}) custom-call(s32[92]{0:T(128)} %copy-done.7, f32[20,1]{1,0:T(8,128)} %copy.17.scale_ref, f32[8,40,768]{2,1,0:T(8,128)} %copy-done.3, bf16[180,64800]{1,0:T(8,128)(2,1)} %refs_1_.3, bf16[180,64800]{1,0:T(8,128)(2,1)} %refs_2_.5, bf16[180,128]{1,0:T(8,128)(2,1)} %pad.7.refs_4_.refs_3_, ...), custom_call_target="tpu_custom_call" | custom-call | bytes 43200000 | tf_op jit(solution)/shard_map/legendre/pallas_call | solution.py:457
  264.1 2.1 add.48
  270.2 2.4 collective-permute-done.1
  272.6 1.3 fusion
  274.3 1.3 add.51
  275.7 1.6 collective-permute-start.5
  277.2 12.3 %collective-permute-done.3 = f32[8,32,768]{2,1,0:T(8,128)} collective-permute-done((f32[8,32,768]{2,1,0:T(8,128)}, f32[8,32,768]{2,1,0:T(8,128)}, u32[]{:S(2)}, u32[]{:S(2)}) %collective-permute-start.3) | collective-permute-done | bytes 786464 | tf_op jit(solution)/shard_map/ppermute | solution.py:479
  291.0 8.5 %collective-permute-done.5 = f32[5,32,768]{2,1,0:T(8,128)S(1)} collective-permute-done((f32[5,32,768]{2,1,0:T(8,128)S(1)}, f32[5,32,768]{2,1,0:T(8,128)S(1)}, u32[]{:S(2)}, u32[]{:S(2)}) %collective-permute-start.5) | collective-permute-done | bytes 491552 | tf_op jit(solution)/shard_map/ppermute | solution.py:479
  (61 shorter events, 15.0 us)
Async XLA Ops:
  6.1 44.3 %all-to-all-start = ((f32[8,6,64,128]{3,2,1,0:T(8,128)}), f32[8,6,64,128]{3,2,1,0:T(8,128)S(1)}, u32[]{:S(2)}, u32[]{:S(2)}) async-start(f32[8,6,64,128]{3,2,1,0:T(8,128)} %eddy_flux.2), calls=%async_computation | async-start | bytes 3145728 | tf_op jit(solution)/shard_map/all_to_all | solution.py:494
  50.3 1.2 copy-start
  51.5 70.4 %all-to-all-start.1 = ((f32[8,6,120,128]{3,2,1,0:T(8,128)}), f32[8,6,120,128]{3,2,1,0:T(8,128)}, u32[]{:S(2)}, u32[]{:S(2)}) async-start(f32[8,6,120,128]{3,2,1,0:T(8,128)} %eddy_flux.3), calls=%async_computation.1 | async-start | bytes 5898240 | tf_op jit(solution)/shard_map/all_to_all | solution.py:494
  122.0 21.1 %all-to-all-start.2 = ((f32[8,80,256]{2,1,0:T(8,128)}), f32[8,80,256]{2,1,0:T(8,128)S(1)}, u32[]{:S(2)}, u32[]{:S(2)}) async-start(f32[8,80,256]{2,1,0:T(8,128)} %dft.4), calls=%async_computation.2 | async-start | bytes 1310720 | tf_op jit(solution)/shard_map/all_to_all | solution.py:494
  143.1 3.8 %copy-start.4 = (f32[8,80,256]{2,1,0:T(8,128)}, f32[8,80,256]{2,1,0:T(8,128)S(1)}, u32[]{:S(2)}) copy-start(f32[8,80,256]{2,1,0:T(8,128)S(1)} %all-to-all-done.2.refs_0_) | copy-start | bytes 1966084
  143.1 35.2 %all-to-all-start.3 = ((f32[8,80,512]{2,1,0:T(8,128)}), f32[8,80,512]{2,1,0:T(8,128)S(1)}, u32[]{:S(2)}, u32[]{:S(2)}) async-start(f32[8,80,512]{2,1,0:T(8,128)} %dft.5), calls=%async_computation.3 | async-start | bytes 2621440 | tf_op jit(solution)/shard_map/all_to_all | solution.py:494
  155.2 27.8 %copy-start.8 = (s32[90]{0:T(128)S(1)}, s32[90]{0:T(128)}, u32[]{:S(2)}) copy-start(s32[90]{0:T(128)} %param.15) | copy-start | bytes 1084
  155.2 27.9 %copy-start.10 = (s32[92]{0:T(128)S(1)}, s32[92]{0:T(128)}, u32[]{:S(2)}) copy-start(s32[92]{0:T(128)} %constant.51) | copy-start | bytes 1108
  155.2 29.9 %slice-start = ((bf16[180,64800]{1,0:T(8,128)(2,1)}), bf16[180,32]{1,0:T(8,128)(2,1)S(1)}, s32[]{:S(2)}) async-start(bf16[180,64800]{1,0:T(8,128)(2,1)} %refs_1_.3), calls=%async_computation.6 | async-start | bytes 94208 | tf_op jit(solution)/shard_map/slice | solution.py:514
  155.2 30.5 %slice-start.1 = ((bf16[180,64800]{1,0:T(8,128)(2,1)}), bf16[180,32]{1,0:T(8,128)(2,1)S(1)}, s32[]{:S(2)}) async-start(bf16[180,64800]{1,0:T(8,128)(2,1)} %refs_2_.5), calls=%async_computation.7 | async-start | bytes 94208 | tf_op jit(solution)/shard_map/slice | solution.py:514
  178.3 1.1 copy-start.2
  179.4 40.8 %all-to-all-start.4 = ((f32[8,64,768]{2,1,0:T(8,128)}), f32[8,64,768]{2,1,0:T(8,128)S(1)}, u32[]{:S(2)}, u32[]{:S(2)}) async-start(f32[8,64,768]{2,1,0:T(8,128)} %dft.6), calls=%async_computation.4 | async-start | bytes 3145728 | tf_op jit(solution)/shard_map/all_to_all | solution.py:494
  184.3 2.0 copy-start.7
  211.1 33.8 %collective-permute-start = (f32[20,32,768]{2,1,0:T(8,128)}, f32[20,32,768]{2,1,0:T(8,128)}, u32[]{:S(2)}, u32[]{:S(2)}) collective-permute-start(f32[20,32,768]{2,1,0:T(8,128)} %get-tuple-element.36), channel_id=1, source_target_pairs={{0,1},{1,0},{2,3},{3,2},{4,5},{5,4},{6,7},{7,6},{8,9},{9,8},{10,11... | collective-permute-start | bytes 5898248 | tf_op jit(solution)/shard_map/ppermute | solution.py:479
  220.2 4.5 %copy-start.1 = (f32[8,64,768]{2,1,0:T(8,128)}, f32[8,64,768]{2,1,0:T(8,128)S(1)}, u32[]{:S(2)}) copy-start(f32[8,64,768]{2,1,0:T(8,128)S(1)} %all-to-all-done.4.refs_0_) | copy-start | bytes 4718596
  220.2 29.9 %all-to-all-start.5 = ((f32[8,40,768]{2,1,0:T(8,128)}), f32[8,40,768]{2,1,0:T(8,128)S(1)}, u32[]{:S(2)}, u32[]{:S(2)}) async-start(f32[8,40,768]{2,1,0:T(8,128)} %dft.7), calls=%async_computation.5 | async-start | bytes 1966080 | tf_op jit(solution)/shard_map/all_to_all | solution.py:494
  224.7 20.2 %copy-start.5 = (f32[20,32,768]{2,1,0:T(8,128)S(1)}, f32[20,32,768]{2,1,0:T(8,128)}, u32[]{:S(2)}) copy-start(f32[20,32,768]{2,1,0:T(8,128)} %get-tuple-element.35) | copy-start | bytes 5898244
  244.8 19.3 %collective-permute-start.2 = (f32[16,32,768]{2,1,0:T(8,128)}, f32[16,32,768]{2,1,0:T(8,128)}, u32[]{:S(2)}, u32[]{:S(2)}) collective-permute-start(f32[16,32,768]{2,1,0:T(8,128)} %get-tuple-element.41), channel_id=1, source_target_pairs={{0,1},{1,0},{2,3},{3,2},{4,5},{5,4},{6,7},{7,6},{8,9},{9,8},{10,11... | collective-permute-start | bytes 4718600 | tf_op jit(solution)/shard_map/ppermute | solution.py:479
  247.8 24.9 %collective-permute-start.1 = (f32[10,32,768]{2,1,0:T(8,128)}, f32[10,32,768]{2,1,0:T(8,128)}, u32[]{:S(2)}, u32[]{:S(2)}) collective-permute-start(f32[10,32,768]{2,1,0:T(8,128)} %slice_bitcast_fusion), channel_id=1, source_target_pairs={{0,2},{1,3},{2,0},{3,1},{4,6},{5,7},{6,4},{7,5},{8,10},{9,11},{10,... | collective-permute-start | bytes 2949128 | tf_op jit(solution)/shard_map/ppermute | solution.py:479
  250.0 1.0 copy-start.3
  263.8 10.5 %collective-permute-start.4 = (f32[10,32,768]{2,1,0:T(8,128)}, f32[10,32,768]{2,1,0:T(8,128)}, u32[]{:S(2)}, u32[]{:S(2)}) collective-permute-start(f32[10,32,768]{2,1,0:T(8,128)} %get-tuple-element.46), channel_id=1, source_target_pairs={{0,1},{1,0},{2,3},{3,2},{4,5},{5,4},{6,7},{7,6},{8,9},{9,8},{10,11... | collective-permute-start | bytes 2949128 | tf_op jit(solution)/shard_map/ppermute | solution.py:479
  266.1 1.5 copy-start.11
  267.1 6.8 %copy-start.9 = (s32[16]{0:T(128)S(1)}, s32[16]{0:T(128)}, u32[]{:S(2)}) copy-start(s32[16]{0:T(128)} %lev_ref.3) | copy-start | bytes 196
  267.1 22.4 %collective-permute-start.3 = (f32[8,32,768]{2,1,0:T(8,128)}, f32[8,32,768]{2,1,0:T(8,128)}, u32[]{:S(2)}, u32[]{:S(2)}) collective-permute-start(f32[8,32,768]{2,1,0:T(8,128)} %slice_bitcast_fusion.2), channel_id=1, source_target_pairs={{0,2},{1,3},{2,0},{3,1},{4,6},{5,7},{6,4},{7,5},{8,10},{9,11},{10,... | collective-permute-start | bytes 2359304 | tf_op jit(solution)/shard_map/ppermute | solution.py:479
  270.2 4.1 %copy-start.6 = (f32[10,32,768]{2,1,0:T(8,128)S(1)}, f32[10,32,768]{2,1,0:T(8,128)}, u32[]{:S(2)}) copy-start(f32[10,32,768]{2,1,0:T(8,128)} %get-tuple-element.45) | copy-start | bytes 2949124
  275.7 23.8 %collective-permute-start.5 = (f32[5,32,768]{2,1,0:T(8,128)S(1)}, f32[5,32,768]{2,1,0:T(8,128)S(1)}, u32[]{:S(2)}, u32[]{:S(2)}) collective-permute-start(f32[5,32,768]{2,1,0:T(8,128)S(1)} %slice_bitcast_fusion.4), channel_id=1, source_target_pairs={{0,2},{1,3},{2,0},{3,1},{4,6},{5,7},{6,4},{7,5},{8,10},{9,11},{10,... | collective-permute-start | bytes 1474568 | tf_op jit(solution)/shard_map/ppermute | solution.py:479

commit v3 on v2

--- a/solution.py
+++ b/solution.py
@@ -18,7 +18,7 @@
 LANES = 128
 HALF = 64
 VMEM_LIMIT = 56 * 1024 * 1024
-PARTS = (10, 8, 5)
+PARTS = (9, 9, 5)
 
 
 def up(value, step):

time: 302 us -> 305 us (level)
  transfers between devices with their start and end apart: 12 -> 12, of which waited for: 8 -> 7; matrix products, arithmetic and copies ran while one was open for 5% -> 5% of each run, Pallas kernels for 37% -> 38%
where the time goes in v3:
time: 305 us; the launch traced here: 304 us
  waiting for transfers between devices  131 us (43%)
  Pallas kernels  120 us (39%)
  starting transfers between devices  30.5 us (10%)
  local copies, waits for them, and re-layouts  11.7 us (4%)
  other arithmetic  7.54 us (2%)
    all_to_all x6, waiting for transfers between devices, exchange(): return lax.all_to_all(x, 'lon', 0, 0, tiled=True)  108 us
    pallas_call x3, Pallas kernels, legendre_call(): pl.pallas_call(functools.partial(legendre_kernel, plan, part, wide, buffe...  58.1 us
    pallas_call x4, Pallas kernels, dft_call(): pl.pallas_call(functools.partial(dft_kernel, plan), out_shape=jax.ShapeDt...  27.2 us
    all_to_all x6, starting transfers between devices, exchange(): return lax.all_to_all(x, 'lon', 0, 0, tiled=True)  26.5 us
    ppermute x6, waiting for transfers between devices, reduce_scatter(): lax.ppermute(send, 'lat', [(t, t ^ bit) for t in range(plan.lat_count)])  23.3 us
    pallas_call x2, Pallas kernels, flux_call(): pl.pallas_call(functools.partial(flux_kernel, plan, group), grid=(pl.cdiv...  15.1 us
    pallas_call x1, Pallas kernels, table_call(): pl.pallas_call(functools.partial(table_kernel, plan), grid=(1,), in_specs...  12.8 us
    add x6, other arithmetic, reduce_scatter(): total = keep + got  7.38 us
  transfers between devices with their start and end apart: 12, of which 7 were waited for; matrix products, arithmetic and copies ran while one was open for 5% of the time, Pallas kernels for 38%

profile of v3, /device:TPU:0, one launch (start us, length us, event | category | flops | bytes accessed | tf_op | source)
XLA Modules:
  0.0 303.6 jit_solution(16906158004264921840)
XLA Ops:
  0.0 6.0 %eddy_flux.2 = f32[8,6,64,128]{3,2,1,0:T(8,128)} custom-call(s32[16]{0:T(128)} %lev_ref.3, s32[1,90]{1,0:T(1,128)} %bitcast.51, f32[128,90]{1,0:T(8,128)} %constant.35.clone.pick_ref, f32[128,1]{1,0:T(8,128)} %constant.36.clone.absent_ref, f32[180,16,180]{2,1,0:T(8,128)} %bitcast.39, f32[180,16,180]{2,1,0:T(8,128)} %bitcast.41, f32[180,16,180]{2,1,0:T(8,128)} %bitcast.43), custom_call_target="tpu_custom_call" | custom-call | bytes 19200000 | tf_op jit(solution)/shard_map/eddy_flux/pallas_call | solution.py:160
  6.0 7.3 %all-to-all-start = ((f32[8,6,64,128]{3,2,1,0:T(8,128)}), f32[8,6,64,128]{3,2,1,0:T(8,128)S(1)}, u32[]{:S(2)}, u32[]{:S(2)}) async-start(f32[8,6,64,128]{3,2,1,0:T(8,128)} %eddy_flux.2), calls=%async_computation | async-start | bytes 3145728 | tf_op jit(solution)/shard_map/all_to_all | solution.py:494
  13.3 9.1 %eddy_flux.3 = f32[8,6,120,128]{3,2,1,0:T(8,128)} custom-call(s32[16]{0:T(128)} %lev_ref.3, s32[1,90]{1,0:T(1,128)} %bitcast.52, f32[128,90]{1,0:T(8,128)} %constant.35.clone.pick_ref, f32[128,1]{1,0:T(8,128)} %constant.36.clone.absent_ref, f32[180,16,180]{2,1,0:T(8,128)} %bitcast.40, f32[180,16,180]{2,1,0:T(8,128)} %bitcast.42, f32[180,16,180]{2,1,0:T(8,128)} %bitcast.44), custom_call_target="tpu_custom_call" | custom-call | bytes 34800000 | tf_op jit(solution)/shard_map/eddy_flux/pallas_call | solution.py:160
  22.4 27.9 %all-to-all-done.got_ref = f32[8,6,64,128]{3,2,1,0:T(8,128)S(1)} async-done(((f32[8,6,64,128]{3,2,1,0:T(8,128)}), f32[8,6,64,128]{3,2,1,0:T(8,128)S(1)}, u32[]{:S(2)}, u32[]{:S(2)}) %all-to-all-start) | async-done | bytes 1572896 | tf_op jit(solution)/shard_map/all_to_all | solution.py:494
  51.5 4.4 %all-to-all-start.1 = ((f32[8,6,120,128]{3,2,1,0:T(8,128)}), f32[8,6,120,128]{3,2,1,0:T(8,128)}, u32[]{:S(2)}, u32[]{:S(2)}) async-start(f32[8,6,120,128]{3,2,1,0:T(8,128)} %eddy_flux.3), calls=%async_computation.1 | async-start | bytes 5898240 | tf_op jit(solution)/shard_map/all_to_all | solution.py:494
  56.0 12.8 %wave_table.1 = (bf16[8,72,1536]{2,1,0:T(8,128)(2,1)}, bf16[8,72,1536]{2,1,0:T(8,128)(2,1)}, bf16[8,40,1536]{2,1,0:T(8,128)(2,1)}, bf16[8,72,1536]{2,1,0:T(8,128...) custom-call(f32[8,6,64,128]{3,2,1,0:T(8,128)} %copy-done), custom_call_target="tpu_custom_call" | custom-call | bytes 43200000 | tf_op jit(solution)/shard_map/wave_table/pallas_call | solution.py:238
  68.7 2.8 split_circles.2
  71.5 4.8 %dft.4 = f32[8,72,256]{2,1,0:T(8,128)} custom-call(bf16[8,72,1536]{2,1,0:T(8,128)(2,1)} %get-tuple-element.26.th_ref, bf16[8,72,1536]{2,1,0:T(8,128)(2,1)} %get-tuple-element.27.tl_ref, bf16[256,1536]{1,0:T(8,128)(2,1)} %get-tuple-element.28.refs_0_, bf16[256,1536]{1,0:T(8,128)(2,1)} %get-tuple-element.29.refs_1_), custom_call_target="tpu_custom_call" | custom-call | bytes 12678260 | tf_op jit(solution)/shard_map/dft/pallas_call | solution.py:311
  76.3 45.6 %all-to-all-done.1.got_ref = f32[8,6,120,128]{3,2,1,0:T(8,128)} async-done(((f32[8,6,120,128]{3,2,1,0:T(8,128)}), f32[8,6,120,128]{3,2,1,0:T(8,128)}, u32[]{:S(2)}, u32[]{:S(2)}) %all-to-all-start.1) | async-done | bytes 2949152 | tf_op jit(solution)/shard_map/all_to_all | solution.py:494
  121.9 3.6 %all-to-all-start.2 = ((f32[8,72,256]{2,1,0:T(8,128)}), f32[8,72,256]{2,1,0:T(8,128)S(1)}, u32[]{:S(2)}, u32[]{:S(2)}) async-start(f32[8,72,256]{2,1,0:T(8,128)} %dft.4), calls=%async_computation.2 | async-start | bytes 1179648 | tf_op jit(solution)/shard_map/all_to_all | solution.py:494
  125.6 3.9 %split_circles.3 = (bf16[512,1536]{1,0:T(8,128)(2,1)}, bf16[512,1536]{1,0:T(8,128)(2,1)}) custom-call(f32[8,6,120,128]{3,2,1,0:T(8,128)} %all-to-all-done.1.got_ref), custom_call_target="tpu_custom_call" | custom-call | bytes 16240000 | tf_op jit(solution)/shard_map/split_circles/pallas_call | solution.py:280
  129.5 6.9 %dft.5 = f32[8,72,512]{2,1,0:T(8,128)} custom-call(bf16[8,72,1536]{2,1,0:T(8,128)(2,1)} %get-tuple-element.26.th_ref, bf16[8,72,1536]{2,1,0:T(8,128)(2,1)} %get-tuple-element.27.tl_ref, bf16[512,1536]{1,0:T(8,128)(2,1)} %get-tuple-element.32.refs_0_.refs_2_, bf16[512,1536]{1,0:T(8,128)(2,1)} %get-tuple-element.33.refs_1_.refs_3_), custom_call_target="tpu_custom_call" | custom-call | bytes 25356520 | tf_op jit(solution)/shard_map/dft/pallas_call | solution.py:311
  136.4 5.2 %all-to-all-done.2.refs_0_ = f32[8,72,256]{2,1,0:T(8,128)S(1)} async-done(((f32[8,72,256]{2,1,0:T(8,128)}), f32[8,72,256]{2,1,0:T(8,128)S(1)}, u32[]{:S(2)}, u32[]{:S(2)}) %all-to-all-start.2) | async-done | bytes 589856 | tf_op jit(solution)/shard_map/all_to_all | solution.py:494
  141.6 3.7 %all-to-all-start.3 = ((f32[8,72,512]{2,1,0:T(8,128)}), f32[8,72,512]{2,1,0:T(8,128)S(1)}, u32[]{:S(2)}, u32[]{:S(2)}) async-start(f32[8,72,512]{2,1,0:T(8,128)} %dft.5), calls=%async_computation.3 | async-start | bytes 2359296 | tf_op jit(solution)/shard_map/all_to_all | solution.py:494
  145.4 9.0 %dft.6 = f32[8,72,768]{2,1,0:T(8,128)} custom-call(bf16[8,72,1536]{2,1,0:T(8,128)(2,1)} %get-tuple-element.37.th_ref, bf16[8,72,1536]{2,1,0:T(8,128)(2,1)} %get-tuple-element.38.tl_ref, bf16[256,1536]{1,0:T(8,128)(2,1)} %get-tuple-element.28.refs_0_, bf16[256,1536]{1,0:T(8,128)(2,1)} %get-tuple-element.29.refs_1_, ...), custom_call_target="tpu_custom_call" | custom-call | bytes 38034784 | tf_op jit(solution)/shard_map/dft/pallas_call | solution.py:311
  154.4 19.6 %all-to-all-done.3.refs_1_ = f32[8,72,512]{2,1,0:T(8,128)S(1)} async-done(((f32[8,72,512]{2,1,0:T(8,128)}), f32[8,72,512]{2,1,0:T(8,128)S(1)}, u32[]{:S(2)}, u32[]{:S(2)}) %all-to-all-start.3) | async-done | bytes 1179680 | tf_op jit(solution)/shard_map/all_to_all | solution.py:494
  175.1 3.6 %all-to-all-start.4 = ((f32[8,72,768]{2,1,0:T(8,128)}), f32[8,72,768]{2,1,0:T(8,128)S(1)}, u32[]{:S(2)}, u32[]{:S(2)}) async-start(f32[8,72,768]{2,1,0:T(8,128)} %dft.6), calls=%async_computation.4 | async-start | bytes 3538944 | tf_op jit(solution)/shard_map/all_to_all | solution.py:494
  182.1 22.2 %legendre.3 = (f32[18,32,768]{2,1,0:T(8,128)}, f32[18,32,768]{2,1,0:T(8,128)}) custom-call(s32[92]{0:T(128)} %copy-done.8, f32[36,1]{1,0:T(8,128)} %copy.15.scale_ref, f32[8,72,256]{2,1,0:T(8,128)} %copy-done.4, f32[8,72,512]{2,1,0:T(8,128)} %copy-done.2, bf16[180,64800]{1,0:T(8,128)(2,1)} %refs_1_.3, bf16[180,64800]{1,0:T(8,128)(2,1)} %refs_2_.5, ...), custom_call_target="tpu_custom_call" | custom-call | bytes 77760000 | tf_op jit(solution)/shard_map/legendre/pallas_call | solution.py:457
  204.4 6.4 %dft.7 = f32[8,40,768]{2,1,0:T(8,128)} custom-call(bf16[8,40,1536]{2,1,0:T(8,128)(2,1)} %get-tuple-element.42.th_ref, bf16[8,40,1536]{2,1,0:T(8,128)(2,1)} %get-tuple-element.43.tl_ref, bf16[256,1536]{1,0:T(8,128)(2,1)} %get-tuple-element.28.refs_0_, bf16[256,1536]{1,0:T(8,128)(2,1)} %get-tuple-element.29.refs_1_, ...), custom_call_target="tpu_custom_call" | custom-call | bytes 21130434 | tf_op jit(solution)/shard_map/dft/pallas_call | solution.py:311
  210.9 9.2 %all-to-all-done.4.refs_0_ = f32[8,72,768]{2,1,0:T(8,128)S(1)} async-done(((f32[8,72,768]{2,1,0:T(8,128)}), f32[8,72,768]{2,1,0:T(8,128)S(1)}, u32[]{:S(2)}, u32[]{:S(2)}) %all-to-all-start.4) | async-done | bytes 1769504 | tf_op jit(solution)/shard_map/all_to_all | solution.py:494
  220.1 3.8 %all-to-all-start.5 = ((f32[8,40,768]{2,1,0:T(8,128)}), f32[8,40,768]{2,1,0:T(8,128)S(1)}, u32[]{:S(2)}, u32[]{:S(2)}) async-start(f32[8,40,768]{2,1,0:T(8,128)} %dft.7), calls=%async_computation.5 | async-start | bytes 1966080 | tf_op jit(solution)/shard_map/all_to_all | solution.py:494
  224.6 22.4 %legendre.4 = (f32[18,32,768]{2,1,0:T(8,128)}, f32[18,32,768]{2,1,0:T(8,128)}) custom-call(s32[92]{0:T(128)} %copy-done.8, f32[36,1]{1,0:T(8,128)} %copy.16.scale_ref, f32[8,72,768]{2,1,0:T(8,128)} %copy-done.1, bf16[180,64800]{1,0:T(8,128)(2,1)} %refs_1_.3, bf16[180,64800]{1,0:T(8,128)(2,1)} %refs_2_.5, bf16[180,128]{1,0:T(8,128)(2,1)} %pad.7.refs_4_.refs_3_, ...), custom_call_target="tpu_custom_call" | custom-call | bytes 77760000 | tf_op jit(solution)/shard_map/legendre/pallas_call | solution.py:457
  247.0 1.7 add.45
  249.8 1.5 collective-permute-start.1
  253.0 13.5 %legendre.5 = (f32[10,32,768]{2,1,0:T(8,128)}, f32[10,32,768]{2,1,0:T(8,128)}) custom-call(s32[92]{0:T(128)} %copy-done.8, f32[20,1]{1,0:T(8,128)} %copy.17.scale_ref, f32[8,40,768]{2,1,0:T(8,128)} %copy-done.3, bf16[180,64800]{1,0:T(8,128)(2,1)} %refs_1_.3, bf16[180,64800]{1,0:T(8,128)(2,1)} %refs_2_.5, bf16[180,128]{1,0:T(8,128)(2,1)} %pad.7.refs_4_.refs_3_, ...), custom_call_target="tpu_custom_call" | custom-call | bytes 43200000 | tf_op jit(solution)/shard_map/legendre/pallas_call | solution.py:457
  266.8 1.7 add.48
  272.6 1.3 fusion.1
  274.4 1.3 add.51
  275.7 1.5 collective-permute-start.5
  277.3 15.1 %collective-permute-done.3 = f32[9,32,768]{2,1,0:T(8,128)} collective-permute-done((f32[9,32,768]{2,1,0:T(8,128)}, f32[9,32,768]{2,1,0:T(8,128)}, u32[]{:S(2)}, u32[]{:S(2)}) %collective-permute-start.3) | collective-permute-done | bytes 884768 | tf_op jit(solution)/shard_map/ppermute | solution.py:479
  292.3 1.3 fusion
  293.9 8.2 %collective-permute-done.5 = f32[5,32,768]{2,1,0:T(8,128)S(1)} collective-permute-done((f32[5,32,768]{2,1,0:T(8,128)S(1)}, f32[5,32,768]{2,1,0:T(8,128)S(1)}, u32[]{:S(2)}, u32[]{:S(2)}) %collective-permute-start.5) | collective-permute-done | bytes 491552 | tf_op jit(solution)/shard_map/ppermute | solution.py:479
  (62 shorter events, 13.7 us)
Async XLA Ops:
  6.0 44.3 %all-to-all-start = ((f32[8,6,64,128]{3,2,1,0:T(8,128)}), f32[8,6,64,128]{3,2,1,0:T(8,128)S(1)}, u32[]{:S(2)}, u32[]{:S(2)}) async-start(f32[8,6,64,128]{3,2,1,0:T(8,128)} %eddy_flux.2), calls=%async_computation | async-start | bytes 3145728 | tf_op jit(solution)/shard_map/all_to_all | solution.py:494
  50.3 1.2 copy-start
  51.5 70.4 %all-to-all-start.1 = ((f32[8,6,120,128]{3,2,1,0:T(8,128)}), f32[8,6,120,128]{3,2,1,0:T(8,128)}, u32[]{:S(2)}, u32[]{:S(2)}) async-start(f32[8,6,120,128]{3,2,1,0:T(8,128)} %eddy_flux.3), calls=%async_computation.1 | async-start | bytes 5898240 | tf_op jit(solution)/shard_map/all_to_all | solution.py:494
  121.9 19.7 %all-to-all-start.2 = ((f32[8,72,256]{2,1,0:T(8,128)}), f32[8,72,256]{2,1,0:T(8,128)S(1)}, u32[]{:S(2)}, u32[]{:S(2)}) async-start(f32[8,72,256]{2,1,0:T(8,128)} %dft.4), calls=%async_computation.2 | async-start | bytes 1179648 | tf_op jit(solution)/shard_map/all_to_all | solution.py:494
  141.6 3.8 %copy-start.4 = (f32[8,72,256]{2,1,0:T(8,128)}, f32[8,72,256]{2,1,0:T(8,128)S(1)}, u32[]{:S(2)}) copy-start(f32[8,72,256]{2,1,0:T(8,128)S(1)} %all-to-all-done.2.refs_0_) | copy-start | bytes 1769476
  141.6 32.4 %all-to-all-start.3 = ((f32[8,72,512]{2,1,0:T(8,128)}), f32[8,72,512]{2,1,0:T(8,128)S(1)}, u32[]{:S(2)}, u32[]{:S(2)}) async-start(f32[8,72,512]{2,1,0:T(8,128)} %dft.5), calls=%async_computation.3 | async-start | bytes 2359296 | tf_op jit(solution)/shard_map/all_to_all | solution.py:494
  154.4 24.3 %copy-start.9 = (s32[90]{0:T(128)S(1)}, s32[90]{0:T(128)}, u32[]{:S(2)}) copy-start(s32[90]{0:T(128)} %param.15) | copy-start | bytes 1084
  154.4 24.4 %copy-start.11 = (s32[92]{0:T(128)S(1)}, s32[92]{0:T(128)}, u32[]{:S(2)}) copy-start(s32[92]{0:T(128)} %constant.50) | copy-start | bytes 1108
  154.4 26.4 %slice-start = ((bf16[180,64800]{1,0:T(8,128)(2,1)}), bf16[180,32]{1,0:T(8,128)(2,1)S(1)}, s32[]{:S(2)}) async-start(bf16[180,64800]{1,0:T(8,128)(2,1)} %refs_1_.3), calls=%async_computation.6 | async-start | bytes 94208 | tf_op jit(solution)/shard_map/slice | solution.py:514
  154.4 27.0 %slice-start.1 = ((bf16[180,64800]{1,0:T(8,128)(2,1)}), bf16[180,32]{1,0:T(8,128)(2,1)S(1)}, s32[]{:S(2)}) async-start(bf16[180,64800]{1,0:T(8,128)(2,1)} %refs_2_.5), calls=%async_computation.7 | async-start | bytes 94208 | tf_op jit(solution)/shard_map/slice | solution.py:514
  174.1 1.0 copy-start.2
  175.1 45.0 %all-to-all-start.4 = ((f32[8,72,768]{2,1,0:T(8,128)}), f32[8,72,768]{2,1,0:T(8,128)S(1)}, u32[]{:S(2)}, u32[]{:S(2)}) async-start(f32[8,72,768]{2,1,0:T(8,128)} %dft.6), calls=%async_computation.4 | async-start | bytes 3538944 | tf_op jit(solution)/shard_map/all_to_all | solution.py:494
  180.0 2.1 copy-start.8
  204.3 42.7 %collective-permute-start = (f32[18,32,768]{2,1,0:T(8,128)}, f32[18,32,768]{2,1,0:T(8,128)}, u32[]{:S(2)}, u32[]{:S(2)}) collective-permute-start(f32[18,32,768]{2,1,0:T(8,128)} %get-tuple-element.36), channel_id=1, source_target_pairs={{0,1},{1,0},{2,3},{3,2},{4,5},{5,4},{6,7},{7,6},{8,9},{9,8},{10,11... | collective-permute-start | bytes 5308424 | tf_op jit(solution)/shard_map/ppermute | solution.py:479
  220.1 4.5 %copy-start.1 = (f32[8,72,768]{2,1,0:T(8,128)}, f32[8,72,768]{2,1,0:T(8,128)S(1)}, u32[]{:S(2)}) copy-start(f32[8,72,768]{2,1,0:T(8,128)S(1)} %all-to-all-done.4.refs_0_) | copy-start | bytes 5308420
  220.1 31.9 %all-to-all-start.5 = ((f32[8,40,768]{2,1,0:T(8,128)}), f32[8,40,768]{2,1,0:T(8,128)S(1)}, u32[]{:S(2)}, u32[]{:S(2)}) async-start(f32[8,40,768]{2,1,0:T(8,128)} %dft.7), calls=%async_computation.5 | async-start | bytes 1966080 | tf_op jit(solution)/shard_map/all_to_all | solution.py:494
  224.6 22.5 %copy-start.6 = (f32[18,32,768]{2,1,0:T(8,128)S(1)}, f32[18,32,768]{2,1,0:T(8,128)}, u32[]{:S(2)}) copy-start(f32[18,32,768]{2,1,0:T(8,128)} %get-tuple-element.35) | copy-start | bytes 5308420
  246.9 19.9 %collective-permute-start.2 = (f32[18,32,768]{2,1,0:T(8,128)}, f32[18,32,768]{2,1,0:T(8,128)}, u32[]{:S(2)}, u32[]{:S(2)}) collective-permute-start(f32[18,32,768]{2,1,0:T(8,128)} %get-tuple-element.41), channel_id=1, source_target_pairs={{0,1},{1,0},{2,3},{3,2},{4,5},{5,4},{6,7},{7,6},{8,9},{9,8},{10,11... | collective-permute-start | bytes 5308424 | tf_op jit(solution)/shard_map/ppermute | solution.py:479
  249.8 22.9 %collective-permute-start.1 = (f32[9,32,768]{2,1,0:T(8,128)}, f32[9,32,768]{2,1,0:T(8,128)}, u32[]{:S(2)}, u32[]{:S(2)}) collective-permute-start(f32[9,32,768]{2,1,0:T(8,128)} %slice_bitcast_fusion.2), channel_id=1, source_target_pairs={{0,2},{1,3},{2,0},{3,1},{4,6},{5,7},{6,4},{7,5},{8,10},{9,11},{10,... | collective-permute-start | bytes 2654216 | tf_op jit(solution)/shard_map/ppermute | solution.py:479
  252.0 1.0 copy-start.3
  253.0 13.8 %copy-start.5 = (f32[18,32,768]{2,1,0:T(8,128)S(1)}, f32[18,32,768]{2,1,0:T(8,128)}, u32[]{:S(2)}) copy-start(f32[18,32,768]{2,1,0:T(8,128)} %get-tuple-element.40) | copy-start | bytes 5308420
  266.5 7.8 %collective-permute-start.4 = (f32[10,32,768]{2,1,0:T(8,128)}, f32[10,32,768]{2,1,0:T(8,128)}, u32[]{:S(2)}, u32[]{:S(2)}) collective-permute-start(f32[10,32,768]{2,1,0:T(8,128)} %get-tuple-element.46), channel_id=1, source_target_pairs={{0,1},{1,0},{2,3},{3,2},{4,5},{5,4},{6,7},{7,6},{8,9},{9,8},{10,11... | collective-permute-start | bytes 2949128 | tf_op jit(solution)/shard_map/ppermute | solution.py:479
  268.5 1.6 copy-start.12
  269.6 4.5 %copy-start.10 = (s32[16]{0:T(128)S(1)}, s32[16]{0:T(128)}, u32[]{:S(2)}) copy-start(s32[16]{0:T(128)} %lev_ref.3) | copy-start | bytes 196
  269.6 22.8 %collective-permute-start.3 = (f32[9,32,768]{2,1,0:T(8,128)}, f32[9,32,768]{2,1,0:T(8,128)}, u32[]{:S(2)}, u32[]{:S(2)}) collective-permute-start(f32[9,32,768]{2,1,0:T(8,128)} %slice_bitcast_fusion), channel_id=1, source_target_pairs={{0,2},{1,3},{2,0},{3,1},{4,6},{5,7},{6,4},{7,5},{8,10},{9,11},{10,... | collective-permute-start | bytes 2654216 | tf_op jit(solution)/shard_map/ppermute | solution.py:479
  272.6 1.7 copy-start.7
  275.7 26.4 %collective-permute-start.5 = (f32[5,32,768]{2,1,0:T(8,128)S(1)}, f32[5,32,768]{2,1,0:T(8,128)S(1)}, u32[]{:S(2)}, u32[]{:S(2)}) collective-permute-start(f32[5,32,768]{2,1,0:T(8,128)S(1)} %slice_bitcast_fusion.4), channel_id=1, source_target_pairs={{0,2},{1,3},{2,0},{3,1},{4,6},{5,7},{6,4},{7,5},{8,10},{9,11},{10,... | collective-permute-start | bytes 1474568 | tf_op jit(solution)/shard_map/ppermute | solution.py:479
